TPU v7x, 512 devices: a whole 4x4x16 slice. The times are simulated.
512 devices in a mesh: nodes: 128 (over z, x, core), feat: 4 (over y).
Axes of the slice: x: 4, y: 4, z: 16, core: 2. Of those that a mesh axis runs over, the one named last changes fastest.
Arguments:
- x_t: bfloat16 [128, 16384], P('feat', 'nodes'), may hold values from -6 to 6
- weight: bfloat16 [128, 256], P('feat'), may hold values from -0.5 to 0.5
- block_cols: int32 [128, 16], P('nodes'), may hold values from 0 to 127, as said below
- block_count: int32 [128], P('nodes'), may hold values from 1 to 16, as said below
- block_vals: bfloat16 [128, 16, 128, 128], P('nodes'), may hold values from -0.125 to 0.125
- d_out_t: bfloat16 [256, 16384], P('feat', 'nodes'), may hold values from -6 to 6
Outputs:
- out_t: bfloat16 [256, 16384], P('feat', 'nodes')
- grad_w: float32 [128, 256], P('feat')
- grad_x_t: float32 [128, 16384], P('feat', 'nodes')
Inputs may be any that keep to these rules, and one draw needn't show every extreme that they name: `block_cols`: each row of node blocks names 16 different node blocks. `block_count`: node block 0 has all 16 blocks live.
All inputs are finite; a program needn't handle non-finite values.
Results may differ from a plain program's by a relative error of at most 0.0055.
Values may be sent and summed in bfloat16 or wider, within the bound.
No kernel may reach another device: no remote copies, remote signals or barrier semaphores. Data moves between devices by JAX's collectives and lax.ppermute only.
A program may use at most 64 MiB of HBM per device.

v0:
```python
import jax
import jax.numpy as jnp
from jax import lax
from jax.sharding import PartitionSpec as P


def gelu_fn(value):
    return jax.nn.gelu(value, approximate=True)


def local(x_t, weight, block_cols, block_count, block_vals, d_out_t):
    feat_loc = x_t.shape[0]
    nb_dev = block_cols.shape[0]
    stored = block_cols.shape[1]
    width = block_vals.shape[2]
    rows_dev = nb_dev * width
    node_devs = lax.axis_size("nodes")
    all_blocks = nb_dev * node_devs
    live = jnp.arange(stored)[None, :] < block_count[:, None]
    masked = jnp.where(live[:, :, None, None], block_vals, jnp.zeros_like(block_vals))
    whole = lax.all_gather(x_t, "nodes", axis=1, tiled=True)
    picked = whole.reshape(feat_loc, all_blocks, width)[:, block_cols, :]
    agg = jnp.einsum("fnkj,nkij->fni", picked, masked, preferred_element_type=jnp.float32)
    agg_t = agg.reshape(feat_loc, rows_dev).astype(jnp.bfloat16)
    pre_t = lax.psum_scatter(
        lax.dot_general(
            weight, agg_t, (((0,), (0,)), ((), ())), preferred_element_type=jnp.float32
        ),
        "feat",
        scatter_dimension=0,
        tiled=True,
    )
    out_t = gelu_fn(pre_t).astype(jnp.bfloat16)
    _, pull = jax.vjp(gelu_fn, pre_t)
    grad_pre_t = pull(d_out_t.astype(jnp.float32))[0].astype(jnp.bfloat16)
    full_grad = lax.all_gather(grad_pre_t, "feat", axis=0, tiled=True)
    partial_w = lax.dot_general(
        agg_t, full_grad, (((1,), (1,)), ((), ())), preferred_element_type=jnp.float32
    )
    grad_w = lax.psum(partial_w, "nodes")
    grad_agg_t = jnp.dot(weight, full_grad, preferred_element_type=jnp.float32).astype(jnp.bfloat16)
    contrib = jnp.einsum(
        "fni,nkij->fnkj",
        grad_agg_t.reshape(feat_loc, nb_dev, width),
        masked,
        preferred_element_type=jnp.float32,
    )
    term = jnp.zeros((feat_loc, all_blocks, width), jnp.float32).at[:, block_cols, :].add(contrib)
    received = lax.all_to_all(term, "nodes", split_axis=1, concat_axis=1, tiled=True)
    grad_x_t = jnp.sum(received, axis=1)
    return (out_t, grad_w, grad_x_t)


def solution(mesh):
    return jax.shard_map(
        local,
        mesh=mesh,
        in_specs=(
            P("feat", "nodes"),
            P("feat", None),
            P("nodes", None),
            P("nodes"),
            P("nodes", None, None, None),
            P("feat", "nodes"),
        ),
        out_specs=(P("feat", "nodes"), P("feat", None), P("feat", "nodes")),
        check_vma=False,
    )
```

profile of v0, /device:TPU:1, one launch (start us, length us, event | category | flops | bytes accessed | tf_op | source)
XLA Modules:
  0.0 787.6 jit_solution(6884561396617127588)
XLA Ops:
  7.2 0.0 copy-start
  7.2 0.0 copy-start.1
  7.2 0.0 copy-start.2
  7.2 0.0 all-gather.2.cloned.1.call-start
  7.2 0.7 all-gather.2.cloned.1.call-update
  7.9 0.0 reduce-scatter.4.cloned.1.call-start
  8.6 0.7 fusion.16
  9.3 138.1 %all-gather.2.cloned.1.call-done = bf16[32,16384]{1,0:T(8,128)(2,1)} async-done(((bf16[32,128]{1,0:T(8,128)(2,1)}), bf16[32,16384]{1,0:T(8,128)(2,1)}) %all-gather.2.cloned.1.call-update) | async-done | bytes 1048592 | tf_op jit(solution)/shard_map/all_gather | solution.py:21
  147.4 1.4 copy_bitcast_fusion
  148.8 0.6 gather_fusion
  149.4 0.0 copy-done.1
  149.4 0.3 fusion.2
  149.8 0.0 copy-done
  149.8 0.2 convolution_bitcast_fusion.1
  150.0 0.8 copy.27
  150.7 0.0 reduce-scatter.4.cloned.1.call-update
  150.7 21.3 %reduce-scatter.4.cloned.1.call-done = f32[64,128]{1,0:T(8,128)} async-done(((f32[256,128]{1,0:T(8,128)}), f32[64,128]{1,0:T(8,128)}) %reduce-scatter.4.cloned.1.call-update) | async-done | bytes 32784 | tf_op jit(solution)/shard_map/reduce_scatter | solution.py:25
  172.0 0.0 copy-done.2
  172.0 1.4 fusion.8
  173.4 9.0 %all_gather.7 = bf16[256,128]{1,0:T(8,128)(2,1)S(1)} all-gather(bf16[64,128]{1,0:T(8,128)(2,1)S(1)} %get-tuple-element.15), channel_id=1, replica_groups=mesh['nodes'=128,'feat'=4] {'feat'}, dimensions={0}, use_global_device_ids=true | all-gather | bytes 81920 | tf_op jit(solution)/shard_map/all_gather | solution.py:36
  182.4 0.3 convolution_bitcast_fusion
  182.7 1.6 broadcast_in_dim.24
  184.3 2.4 scatter_fusion
  186.7 21.7 %all-to-all-start = ((f32[32,128,128]{2,0,1:T(8,128)}), f32[32,128,128]{2,0,1:T(8,128)S(1)}, u32[]{:S(2)}, u32[]{:S(2)}) async-start(f32[32,128,128]{2,0,1:T(8,128)} %scatter_fusion), calls=%async_computation | async-start | bytes 4194304 | tf_op jit(solution)/shard_map/all_to_all | solution.py:49
  208.5 0.1 fusion.19
  208.6 571.4 %psum.7 = f32[32,256]{1,0:T(8,128)} all-reduce(f32[32,256]{1,0:T(8,128)S(1)} %fusion.19), channel_id=1, replica_groups=mesh['nodes'=128,'feat'=4] {'nodes'}, use_global_device_ids=true, to_apply=%region_1.2 | all-reduce | flops 8192 | bytes 65536 | tf_op jit(solution)/shard_map/psum | solution.py:40
  779.9 0.0 all-to-all-done
  779.9 0.8 reduce_sum.9
  (2 shorter events, 0.0 us)
Async XLA Ops:
  7.2 142.6 %copy-start = (bf16[32,256]{1,0:T(8,128)(2,1)S(1)}, bf16[32,256]{1,0:T(8,128)(2,1)}, u32[]{:S(2)}) copy-start(bf16[32,256]{1,0:T(8,128)(2,1)} %param.7) | copy-start | bytes 49156
  7.2 142.2 %copy-start.1 = (bf16[1,16,128,128]{3,2,1,0:T(8,128)(2,1)S(1)}, bf16[1,16,128,128]{3,2,1,0:T(8,128)(2,1)}, u32[]{:S(2)}) copy-start(bf16[1,16,128,128]{3,2,1,0:T(8,128)(2,1)} %param.10) | copy-start | bytes 1572868
  7.2 164.8 %copy-start.2 = (bf16[64,128]{1,0:T(8,128)(2,1)S(1)}, bf16[64,128]{1,0:T(8,128)(2,1)}, u32[]{:S(2)}) copy-start(bf16[64,128]{1,0:T(8,128)(2,1)} %param.11) | copy-start | bytes 49156
  7.2 140.2 %all-gather.2.cloned.1.call-start = ((), (), s32[]{:S(2)}) async-start(), calls=%async_computation.2 | async-start | bytes 1056768 | tf_op jit(solution)/shard_map/all_gather | solution.py:21
  7.9 164.1 %reduce-scatter.4.cloned.1.call-start = ((), (), s32[]{:S(2)}) async-start(), calls=%async_computation.3 | async-start | bytes 163840 | tf_op jit(solution)/shard_map/reduce_scatter | solution.py:25
  186.7 593.2 %all-to-all-start = ((f32[32,128,128]{2,0,1:T(8,128)}), f32[32,128,128]{2,0,1:T(8,128)S(1)}, u32[]{:S(2)}, u32[]{:S(2)}) async-start(f32[32,128,128]{2,0,1:T(8,128)} %scatter_fusion), calls=%async_computation | async-start | bytes 4194304 | tf_op jit(solution)/shard_map/all_to_all | solution.py:49
Sparse Core Ops, SparseCore 0:
  11.0 136.3 all-gather.1
  150.9 21.0 reduce-scatter.3
where the time goes:
time: 791 us; the launch traced here: 788 us
  blocking collectives  580 us (73%)
  waiting for transfers between devices  160 us (20%)
  starting transfers between devices  21.8 us (3%)
  between operations  14.8 us (2%)
    psum x1, blocking collectives, local(): grad_w = lax.psum(partial_w, 'nodes')  571 us
    all_gather x1, waiting for transfers between devices, local(): whole = lax.all_gather(x_t, 'nodes', axis=1, tiled=True)  138 us
    all_to_all x1, starting transfers between devices, local(): lax.all_to_all(term, 'nodes', split_axis=1, concat_axis=1, tiled=True)  21.7 us
    reduce_scatter x1, waiting for transfers between devices, local(): lax.psum_scatter(lax.dot_general(weight, agg_t, (((0,), (0,)), ((), ())),...  21.3 us
  transfers between devices with their start and end apart: 3, of which 2 were waited for; matrix products, arithmetic and copies ran while one was open for 0% of the time, Pallas kernels for 0%

commit v1 on v0

v1 whole, which is shorter than its diff:
```python
import jax
import jax.numpy as jnp
from jax import lax
from jax.experimental import pallas as pl
from jax.experimental.pallas import tpu as pltpu
from jax.sharding import Mesh, PartitionSpec as P

BF = jnp.bfloat16
F32 = jnp.float32
NZ, NX, NC, NY = 16, 4, 2, 4
K, B, FL, HL = 16, 128, 32, 64
QK = K // NY
D_AT, W_AT = QK * B, QK * B + HL
ROWS = W_AT + 2 * FL
PACK = FL + 2 * B + FL
C0, C1 = 0.7978845608, 0.044715
VM = pltpu.CompilerParams(vmem_limit_bytes=32 * 1024 * 1024)
VMEM = pl.BlockSpec(memory_space=pltpu.VMEM)
SMEM = pl.BlockSpec(memory_space=pltpu.SMEM)


def dot(a, b, ca, cb):
    return lax.dot_general(a, b, (((ca,), (cb,)), ((), ())), preferred_element_type=F32)


def agg_kernel(idx, ids, xg, g, out):
    core = ids[0]
    for r in range(NC):
        acc = jnp.zeros((FL, B), F32)
        for s in range(K):
            owner = idx[r, s]
            use = jnp.logical_and(owner % NC == core, s < idx[r, K])
            got = xg[(owner // NC) % NX, owner // (NC * NX)]
            got = jnp.where(use, got, jnp.zeros_like(got))
            vals = g[r * NY + s // QK, (s % QK) * B : (s % QK + 1) * B, :]
            acc = acc + dot(got, vals, 1, 1)
        for y in range(NY):
            out[r * NY + y] = acc


def mid_kernel(ids, parts, g, out_t, pack):
    core, y_at = ids[0], ids[1]
    agg = [(parts[y] + parts[NY + y]).astype(BF) for y in range(NY)]
    agg_all = jnp.concatenate(agg, axis=0)
    for h in range(2):
        w = jnp.concatenate(
            [g[y, W_AT + h * FL : W_AT + (h + 1) * FL, :] for y in range(NY)], axis=0
        )
        pre = dot(w, agg_all, 0, 0)
        t = jnp.tanh(C0 * (pre + C1 * (pre * pre * pre)))
        val = (0.5 * pre * (1.0 + t)).astype(BF)
        der = 0.5 * (1.0 + t) + 0.5 * pre * (1.0 - t * t) * (C0 * (1.0 + 3.0 * C1 * (pre * pre)))
        for q in range(2):
            y = 2 * h + q

            @pl.when(y_at == y)
            def _():
                out_t[...] = val[q * HL : (q + 1) * HL]

            cot = g[core * NY + y, D_AT : D_AT + HL, :].astype(F32)
            at = FL + y * HL
            pack[at : at + HL, :] = (cot * der[q * HL : (q + 1) * HL]).astype(BF)
    own = sum(jnp.where(y_at == y, (parts[y] + parts[NY + y]), 0.0) for y in range(NY))
    pack[0:FL, :] = own.astype(BF)
    back = jnp.zeros((FL, B), F32)
    for h in range(2):
        w_own = g[y_at, W_AT + h * FL : W_AT + (h + 1) * FL, :]
        back = back + dot(w_own, pack[FL + h * B : FL + (h + 1) * B, :], 1, 0)
    pack[FL + 2 * B : PACK, :] = back.astype(BF)


def back_kernel(idx, ids, both, g, out, term):
    core = ids[0]
    term[...] = jnp.zeros_like(term)
    gw = jnp.zeros((FL, B), F32)
    for r in range(NC):
        half = both[r, pl.ds(pl.multiple_of(FL + core * B, FL), B), :]
        gw = gw + dot(both[r, 0:FL, :], half, 1, 1)
        grad = both[r, FL + 2 * B : PACK, :]
        for s in range(K):
            owner = idx[r, s]
            use = jnp.logical_and(owner % NC == core, s < idx[r, K])
            at = ((owner // NC) % NX) * NZ + owner // (NC * NX)
            at = jnp.where(use, at, NX * NZ)
            vals = g[r * NY + s // QK, (s % QK) * B : (s % QK + 1) * B, :]
            term[at] = term[at] + dot(grad, vals, 1, 0)
    gw = gw.astype(BF)
    for x in range(NX):
        for z in range(NZ):
            out[x, z * FL : (z + 1) * FL, :] = term[x * NZ + z].astype(BF)
        out[x, NZ * FL :, :] = gw


def sum_kernel(got, out):
    gw = sum(got[x, NZ * FL :, :].astype(F32) for x in range(NX)).astype(BF)
    for z in range(NZ):
        rows = slice(z * FL, (z + 1) * FL)
        out[z, 0:FL, :] = sum(got[x, rows, :].astype(F32) for x in range(NX)).astype(BF)
        out[z, FL:, :] = gw


def local(x_t, weight, block_cols, block_count, block_vals, d_out_t):
    core, y_at = lax.axis_index("c"), lax.axis_index("y")
    ids = jnp.stack([core, y_at]).astype(jnp.int32)
    with jax.named_scope("gather_small"):
        idx = jnp.concatenate([block_cols, block_count[:, None]], axis=1)
        idx = lax.all_gather(idx, "c", axis=0, tiled=True)
    with jax.named_scope("gather_vals"):
        quarter = lax.dynamic_slice_in_dim(
            block_vals.reshape(K * B, B), y_at * (QK * B), QK * B, axis=0
        )
        mine = jnp.concatenate([quarter, d_out_t, weight[:, :B], weight[:, B:]], axis=0)
        g = lax.all_gather(mine, ("c", "y"), axis=0, tiled=False)
    with jax.named_scope("gather_x"):
        a = lax.all_to_all(jnp.broadcast_to(x_t, (NZ, FL, B)), "z", 0, 0, tiled=True)
        a = lax.all_to_all(jnp.broadcast_to(a, (NX, NZ, FL, B)), "x", 0, 0, tiled=True)
    parts = pl.pallas_call(
        agg_kernel,
        out_shape=jax.ShapeDtypeStruct((NC * NY, FL, B), F32),
        in_specs=[SMEM, SMEM, VMEM, VMEM],
        out_specs=VMEM,
        compiler_params=VM,
        name="agg",
    )(idx, ids, a, g)
    with jax.named_scope("share_agg"):
        parts = lax.all_to_all(parts, ("c", "y"), 0, 0, tiled=True)
    out_t, pack = pl.pallas_call(
        mid_kernel,
        out_shape=(
            jax.ShapeDtypeStruct((HL, B), BF),
            jax.ShapeDtypeStruct((PACK, B), BF),
        ),
        in_specs=[SMEM, VMEM, VMEM],
        out_specs=(VMEM, VMEM),
        compiler_params=VM,
        name="mid",
    )(ids, parts, g)
    with jax.named_scope("share_pair"):
        both = lax.all_gather(pack, "c", axis=0, tiled=False)
    term = pl.pallas_call(
        back_kernel,
        out_shape=jax.ShapeDtypeStruct((NX, NZ * FL + FL, B), BF),
        in_specs=[SMEM, SMEM, VMEM, VMEM],
        out_specs=VMEM,
        scratch_shapes=[pltpu.VMEM((NX * NZ + 1, FL, B), F32)],
        compiler_params=VM,
        name="back",
    )(idx, ids, both, g)
    with jax.named_scope("scatter_x"):
        term = lax.all_to_all(term, "x", 0, 0, tiled=True)
    term = pl.pallas_call(
        sum_kernel,
        out_shape=jax.ShapeDtypeStruct((NZ, 2 * FL, B), BF),
        in_specs=[VMEM],
        out_specs=VMEM,
        compiler_params=VM,
        name="sum_x",
    )(term)
    with jax.named_scope("scatter_z"):
        term = lax.all_to_all(term, "z", 0, 0, tiled=True)
        total = jnp.sum(term.astype(F32), axis=0)
    with jax.named_scope("join_w"):
        grad_w = lax.all_gather(total[FL:], "c", axis=1, tiled=True)
    return (out_t, grad_w, total[:FL])


def solution(mesh):
    fine = Mesh(mesh.devices.reshape(NZ, NX, NC, NY), ("z", "x", "c", "y"))
    nodes = ("z", "x", "c")
    return jax.shard_map(
        local,
        mesh=fine,
        in_specs=(
            P("y", nodes),
            P("y", None),
            P(nodes, None),
            P(nodes),
            P(nodes, None, None, None),
            P("y", nodes),
        ),
        out_specs=(P("y", nodes), P("y", None), P("y", nodes)),
        check_vma=False,
    )
```

time: 791 us -> 118 us (0.15)
  blocking collectives: 580 us -> 86.9 us
  waiting for transfers between devices: 160 us -> 0.75 us
  starting transfers between devices: 21.8 us -> 4.05 us
    psum x1 -> x0, blocking collectives: 571 us -> none  [local(): grad_w = lax.psum(partial_w, 'nodes')]
    all_gather x1, waiting for transfers between devices: 138 us -> 0.01 us  [local(): g = lax.all_gather(mine, ('c', 'y'), axis=0, tiled=False)]
    all_to_all x0 -> x4, blocking collectives: none -> 71.3 us  [the longest x1 27.5 us: local(): lax.all_to_all(jnp.broadcast_to(x_t, (NZ, FL, B)), 'z', 0, 0, tiled=True)]
    reduce_scatter x1 -> x0, waiting for transfers between devices: 21.3 us -> none  [local(): lax.psum_scatter(lax.dot_general(weight, agg_t, (((0,), (0,)), ((), ())),...]
    all_to_all x1, starting transfers between devices: 21.7 us -> 4.01 us  [local(): lax.all_to_all(jnp.broadcast_to(a, (NX, NZ, FL, B)), 'x', 0, 0, tiled=True)]
  transfers between devices with their start and end apart: 3 -> 2, of which waited for: 2 -> 1; matrix products, arithmetic and copies ran while one was open for 0% -> 1% of each run, Pallas kernels for 0% -> 0%
where the time goes in v1:
time: 118 us; the launch traced here: 117 us
  blocking collectives  86.9 us (74%)
  between operations  14.7 us (12%)
  local copies, waits for them, and re-layouts  5.18 us (4%)
  Pallas kernels  4.06 us (3%)
  starting transfers between devices  4.05 us (3%)
  other arithmetic  1.58 us (1%)
    all_to_all x1, blocking collectives, local(): lax.all_to_all(jnp.broadcast_to(x_t, (NZ, FL, B)), 'z', 0, 0, tiled=True)  27.5 us
    all_to_all x1, blocking collectives, local(): term = lax.all_to_all(term, 'z', 0, 0, tiled=True)  17.4 us
    all_to_all x1, blocking collectives, local(): parts = lax.all_to_all(parts, ('c', 'y'), 0, 0, tiled=True)  14.5 us
    all_to_all x1, blocking collectives, local(): term = lax.all_to_all(term, 'x', 0, 0, tiled=True)  11.8 us
    all_gather x1, blocking collectives, local(): grad_w = lax.all_gather(total[FL:], 'c', axis=1, tiled=True)  8.27 us
    all_gather x1, blocking collectives, local(): idx = lax.all_gather(idx, 'c', axis=0, tiled=True)  5.39 us
    all_to_all x1, starting transfers between devices, local(): lax.all_to_all(jnp.broadcast_to(a, (NX, NZ, FL, B)), 'x', 0, 0, tiled=True)  4.01 us
  transfers between devices with their start and end apart: 2, of which 1 were waited for; matrix products, arithmetic and copies ran while one was open for 1% of the time, Pallas kernels for 0%

profile of v1, /device:TPU:1, one launch (start us, length us, event | category | flops | bytes accessed | tf_op | source)
XLA Modules:
  0.0 117.2 jit_solution(11763433438322181495)
XLA Ops:
  7.2 0.0 copy-start
  7.2 0.0 all-gather.5.cloned.1.call-start
  7.2 0.8 fusion.1
  8.0 0.3 copy-done
  8.3 0.0 copy-start.3
  8.3 1.4 %pad_maximum_fusion = bf16[640,128]{1,0:T(8,128)(2,1)} fusion(bf16[32,128]{1,0:T(8,128)(2,1)S(1)} %get-tuple-element.10, bf16[32,128]{1,0:T(8,128)(2,1)S(1)} %get-tuple-element.9, bf16[64,128]{1,0:T(8,128)(2,1)} %param.11, bf16[512,128]{1,0:T(8,128)(2,1)S(1)} %constant_dynamic-slice_fusion), kind=kLoop, calls=%fused_computation.1 | loop fusion | flops 655360 | bytes 327680 | tf_op jit(solution)/shard_map/gather_vals/concatenate | solution.py:112
  9.7 0.0 all-gather.5.cloned.1.call-update
  9.7 0.7 broadcast_in_dim.10
  10.4 27.5 %all_to_all.25 = bf16[16,32,128]{2,1,0:T(8,128)(2,1)S(1)} all-to-all(bf16[16,32,128]{2,1,0:T(8,128)(2,1)S(1)} %broadcast_in_dim.10), channel_id=1, replica_groups=mesh['z'=16,'x'=4,'c'=2,'y'=4] {'z'}, dimensions={0} | all-to-all | bytes 262144 | tf_op jit(solution)/shard_map/gather_x/all_to_all | solution.py:115
  37.9 0.9 broadcast_in_dim.11
  38.8 4.0 %all-to-all-start.1 = ((bf16[4,16,32,128]{3,2,1,0:T(8,128)(2,1)}), bf16[4,16,32,128]{3,2,1,0:T(8,128)(2,1)S(1)}, u32[]{:S(2)}, u32[]{:S(2)}) async-start(bf16[4,16,32,128]{3,2,1,0:T(8,128)(2,1)} %broadcast_in_dim.11), calls=%async_computation.1 | async-start | bytes 1048576 | tf_op jit(solution)/shard_map/gather_x/all_to_all | solution.py:116
  43.5 0.0 copy-done.3
  43.5 0.1 add_bitcast_fusion
  43.6 5.4 %all-gather.2 = s32[2,1,17]{2,1,0:T(1,128)S(1)} all-gather(s32[1,1,17]{2,1,0:T(1,128)S(1)} %add_bitcast_fusion), channel_id=1, replica_groups=mesh['z'=16,'x'=4,'c'=2,'y'=4] {'c'}, dimensions={0}, use_global_device_ids=true | all-gather | bytes 204 | tf_op jit(solution)/shard_map/gather_small/all_gather | solution.py:107
  49.0 0.1 pad_add_fusion.ids
  49.0 0.7 all-to-all-done.1.xg
  49.8 0.0 all-gather.5.cloned.1.call-done
  49.8 0.0 copy-start.1
  49.8 1.3 %copy-done.1 = bf16[5120,128]{1,0:T(8,128)(2,1)S(1)} copy-done((bf16[5120,128]{1,0:T(8,128)(2,1)S(1)}, bf16[5120,128]{1,0:T(8,128)(2,1)}, u32[]{:S(2)}) %copy-start.1) | copy-done | bytes 1310744
  51.1 0.0 copy-start.2
  51.1 1.2 %agg.1 = f32[8,32,128]{2,1,0:T(8,128)S(1)} custom-call(s32[2,17]{1,0:T(2,128)S(1)} %bitcast.15, s32[2]{0:T(128)S(1)} %pad_add_fusion.ids, bf16[4,16,32,128]{3,2,1,0:T(8,128)(2,1)S(1)} %all-to-all-done.1.xg, bf16[8,640,128]{2,1,0:T(8,128)(2,1)S(1)} %bitcast.11), custom_call_target="tpu_custom_call" | custom-call | tf_op jit(solution)/shard_map/agg/pallas_call | solution.py:117
  52.3 14.5 %all_to_all.26.parts = f32[8,32,128]{2,1,0:T(8,128)S(1)} all-to-all(f32[8,32,128]{2,1,0:T(8,128)S(1)} %agg.1), channel_id=1, replica_groups=mesh['z'=16,'x'=4,'c'=2,'y'=4] {'c','y'}, dimensions={0} | all-to-all | bytes 262144 | tf_op jit(solution)/shard_map/share_agg/all_to_all | solution.py:126
  66.8 0.0 copy-done.2
  66.8 1.6 %mid.1 = (bf16[64,128]{1,0:T(8,128)(2,1)}, bf16[320,128]{1,0:T(8,128)(2,1)S(1)}) custom-call(s32[2]{0:T(128)S(1)} %pad_add_fusion.ids, f32[8,32,128]{2,1,0:T(8,128)S(1)} %all_to_all.26.parts, bf16[8,640,128]{2,1,0:T(8,128)(2,1)S(1)} %bitcast.12), custom_call_target="tpu_custom_call" | custom-call | tf_op jit(solution)/shard_map/mid/pallas_call | solution.py:127
  68.4 2.0 %all-gather.1 = bf16[640,128]{1,0:T(8,128)(2,1)S(1)} all-gather(bf16[320,128]{1,0:T(8,128)(2,1)S(1)} %get-tuple-element.6), channel_id=3, replica_groups=mesh['z'=16,'x'=4,'c'=2,'y'=4] {'c'}, dimensions={0}, use_global_device_ids=true | all-gather | bytes 245760 | tf_op jit(solution)/shard_map/share_pair/all_gather | solution.py:139
  70.4 1.2 %back.1 = bf16[4,544,128]{2,1,0:T(8,128)(2,1)S(1)} custom-call(s32[2,17]{1,0:T(2,128)S(1)} %bitcast.16, s32[2]{0:T(128)S(1)} %pad_add_fusion.ids, bf16[2,320,128]{2,1,0:T(8,128)(2,1)S(1)} %bitcast.14, bf16[8,640,128]{2,1,0:T(8,128)(2,1)S(1)} %bitcast.13), custom_call_target="tpu_custom_call" | custom-call | tf_op jit(solution)/shard_map/back/pallas_call | solution.py:140
  71.6 11.8 %all_to_all.27.got = bf16[4,544,128]{2,1,0:T(8,128)(2,1)S(1)} all-to-all(bf16[4,544,128]{2,1,0:T(8,128)(2,1)S(1)} %back.1), channel_id=1, replica_groups=mesh['z'=16,'x'=4,'c'=2,'y'=4] {'x'}, dimensions={0} | all-to-all | bytes 1114112 | tf_op jit(solution)/shard_map/scatter_x/all_to_all | solution.py:150
  83.4 0.1 sum_x.1
  83.4 17.4 %all_to_all.28 = bf16[16,64,128]{2,1,0:T(8,128)(2,1)S(1)} all-to-all(bf16[16,64,128]{2,1,0:T(8,128)(2,1)S(1)} %sum_x.1), channel_id=1, replica_groups=mesh['z'=16,'x'=4,'c'=2,'y'=4] {'z'}, dimensions={0} | all-to-all | bytes 524288 | tf_op jit(solution)/shard_map/scatter_z/all_to_all | solution.py:160
  100.9 0.6 fusion
  101.5 8.3 %all_gather.23 = f32[32,256]{1,0:T(8,128)S(1)} all-gather(f32[32,128]{1,0:T(8,128)S(1)} %get-tuple-element.8), channel_id=1, replica_groups=mesh['z'=16,'x'=4,'c'=2,'y'=4] {'c'}, dimensions={1}, use_global_device_ids=true | all-gather | bytes 49152 | tf_op jit(solution)/shard_map/join_w/all_gather | solution.py:163
  109.8 0.6 copy.11
  (2 shorter events, 0.1 us)
Async XLA Ops:
  7.2 1.1 copy-start
  7.2 42.6 %all-gather.5.cloned.1.call-start = ((), (), s32[]{:S(2)}) async-start(), calls=%async_computation.5 | async-start | bytes 1474560 | tf_op jit(solution)/shard_map/gather_vals/all_gather | solution.py:113
  8.3 35.2 %copy-start.3 = (s32[1,16]{1,0:T(1,128)S(1)}, s32[1,16]{1,0:T(1,128)}, u32[]{:S(2)}) copy-start(s32[1,16]{1,0:T(1,128)} %param.8) | copy-start | bytes 196
  38.8 10.9 %all-to-all-start.1 = ((bf16[4,16,32,128]{3,2,1,0:T(8,128)(2,1)}), bf16[4,16,32,128]{3,2,1,0:T(8,128)(2,1)S(1)}, u32[]{:S(2)}, u32[]{:S(2)}) async-start(bf16[4,16,32,128]{3,2,1,0:T(8,128)(2,1)} %broadcast_in_dim.11), calls=%async_computation.1 | async-start | bytes 1048576 | tf_op jit(solution)/shard_map/gather_x/all_to_all | solution.py:116
  49.8 1.3 %copy-start.1 = (bf16[5120,128]{1,0:T(8,128)(2,1)S(1)}, bf16[5120,128]{1,0:T(8,128)(2,1)}, u32[]{:S(2)}) copy-start(bf16[5120,128]{1,0:T(8,128)(2,1)} %all-gather.5.cloned.1.call-done) | copy-start | bytes 3932164
  51.1 15.7 %copy-start.2 = (bf16[5120,128]{1,0:T(8,128)(2,1)S(1)}, bf16[5120,128]{1,0:T(8,128)(2,1)}, u32[]{:S(2)}) copy-start(bf16[5120,128]{1,0:T(8,128)(2,1)} %all-gather.5.cloned.1.call-done) | copy-start | bytes 3932164
Sparse Core Ops, SparseCore 0:
  10.2 37.2 all-gather.4

commit v2 on v1

v2 whole, which is shorter than its diff:
```python
import jax
import jax.numpy as jnp
from jax import lax
from jax.experimental import pallas as pl
from jax.experimental.pallas import tpu as pltpu
from jax.sharding import Mesh, PartitionSpec as P

BF = jnp.bfloat16
F32 = jnp.float32
NZ, NX, NC, NY = 16, 4, 2, 4
K, B, FL, HL = 16, 128, 32, 64
META = K * B
ROWS = META + 16
RIDE = FL + HL + 2 * FL
PACK = FL + 2 * B + FL
C0, C1 = 0.7978845608, 0.044715
VM = pltpu.CompilerParams(vmem_limit_bytes=32 * 1024 * 1024)
VMEM = pl.BlockSpec(memory_space=pltpu.VMEM)
SMEM = pl.BlockSpec(memory_space=pltpu.SMEM)
HBM = pl.BlockSpec(memory_space=pl.ANY)


def dot(a, b, ca, cb):
    return lax.dot_general(a, b, (((ca,), (cb,)), ((), ())), preferred_element_type=F32)


def call(kernel, outs, name, ins, scratch=()):
    specs, args = zip(*ins)
    one = not isinstance(outs, list)
    shapes = [jax.ShapeDtypeStruct(*o) for o in ((outs,) if one else outs)]
    return pl.pallas_call(
        kernel,
        out_shape=shapes[0] if one else tuple(shapes),
        in_specs=list(specs),
        out_specs=VMEM if one else tuple(VMEM for _ in shapes),
        scratch_shapes=list(scratch),
        compiler_params=VM,
        name=name,
    )(*args)


def prep_kernel(cols, count, x, vals, mine, xb, sem):
    copy = pltpu.make_async_copy(vals, mine.at[0:META], sem)
    copy.start()
    for z in range(NZ):
        xb[z] = x[...]
    lane = lax.broadcasted_iota(jnp.int32, (16, B), 1)
    meta = jnp.where(lane == K, count[0], 0)
    for s in range(K):
        meta = jnp.where(lane == s, cols[0, s], meta)
    mine[META:ROWS, :] = meta.astype(F32).astype(BF)
    copy.wait()


def agg_kernel(mine, peer, xg, out, idx, ints, sem):
    core = lax.axis_index("c")
    idx[0] = mine[META:ROWS, :].astype(F32)[0:8].astype(jnp.int32)
    idx[1] = peer[META:ROWS, :].astype(F32)[0:8].astype(jnp.int32)
    copy = pltpu.make_async_copy(idx, ints, sem)
    copy.start()
    copy.wait()
    for r, blocks in enumerate((mine, peer)):
        acc = jnp.zeros((FL, B), F32)
        for s in range(K):
            owner = ints[r, 0, s]
            use = jnp.logical_and(owner % NC == core, s < ints[r, 0, K])
            got = xg[(owner // NC) % NX, owner // (NC * NX)]
            got = jnp.where(use, got, jnp.zeros_like(got))
            acc = acc + dot(got, blocks[s * B : (s + 1) * B, :], 1, 1)
        out[r] = acc


def ride_kernel(parts, d_out, weight, out):
    core = lax.axis_index("c")
    agg = (parts[core, 0] + parts[1 - core, 1]).astype(BF)
    for y in range(NY):
        out[y, 0:FL, :] = agg
        out[y, FL : FL + HL, :] = d_out[...]
        out[y, FL + HL : 2 * FL + HL, :] = weight[:, :B]
        out[y, 2 * FL + HL :, :] = weight[:, B:]


def mid_kernel(got, out_t, pack):
    y_at = lax.axis_index("y")
    agg = jnp.concatenate([got[y, 0:FL, :] for y in range(NY)], axis=0)
    pack[0:FL, :] = got[y_at, 0:FL, :]
    back = jnp.zeros((FL, B), F32)
    for h in range(2):
        rows = slice(FL + HL + h * FL, FL + HL + (h + 1) * FL)
        w = jnp.concatenate([got[y, rows, :] for y in range(NY)], axis=0)
        pre = dot(w, agg, 0, 0)
        t = jnp.tanh(C0 * (pre + C1 * (pre * pre * pre)))
        val = (0.5 * pre * (1.0 + t)).astype(BF)
        der = 0.5 * (1.0 + t) + 0.5 * pre * (1.0 - t * t) * (C0 * (1.0 + 3.0 * C1 * (pre * pre)))
        for q in range(2):
            y = 2 * h + q

            @pl.when(y_at == y)
            def _():
                out_t[...] = val[q * HL : (q + 1) * HL]

        cot = jnp.concatenate([got[2 * h + q, FL : FL + HL, :] for q in range(2)], axis=0)
        grad = (cot.astype(F32) * der).astype(BF)
        pack[FL + h * B : FL + (h + 1) * B, :] = grad
        back = back + dot(got[y_at, rows, :], grad, 1, 0)
    pack[FL + 2 * B : PACK, :] = back.astype(BF)


def back_kernel(idx, both, mine, peer, out, term):
    core = lax.axis_index("c")
    term[...] = jnp.zeros_like(term)
    gw = jnp.zeros((FL, B), F32)
    for r, blocks in enumerate((mine, peer)):
        row = core if r == 0 else 1 - core
        half = both[row, pl.ds(pl.multiple_of(FL + core * B, FL), B), :]
        gw = gw + dot(both[row, 0:FL, :], half, 1, 1)
        grad = both[row, FL + 2 * B : PACK, :]
        for s in range(K):
            owner = idx[r, 0, s]
            use = jnp.logical_and(owner % NC == core, s < idx[r, 0, K])
            at = ((owner // NC) % NX) * NZ + owner // (NC * NX)
            at = jnp.where(use, at, NX * NZ)
            term[at] = term[at] + dot(grad, blocks[s * B : (s + 1) * B, :], 1, 0)
    gw = gw.astype(BF)
    for x in range(NX):
        for z in range(NZ):
            out[x, z * FL : (z + 1) * FL, :] = term[x * NZ + z].astype(BF)
        out[x, NZ * FL :, :] = gw


def sum_kernel(got, out):
    gw = sum(got[x, NZ * FL :, :].astype(F32) for x in range(NX)).astype(BF)
    for z in range(NZ):
        rows = slice(z * FL, (z + 1) * FL)
        out[z, 0:FL, :] = sum(got[x, rows, :].astype(F32) for x in range(NX)).astype(BF)
        out[z, FL:, :] = gw


def half_kernel(got, out):
    out[...] = sum(got[z, FL:, :].astype(F32) for z in range(NZ))


def last_kernel(got, halves, grad_w, grad_x):
    grad_w[:, :B] = halves[0]
    grad_w[:, B:] = halves[1]
    grad_x[...] = sum(got[z, 0:FL, :].astype(F32) for z in range(NZ))


def local(x_t, weight, block_cols, block_count, block_vals, d_out_t):
    mine, xb = call(
        prep_kernel,
        [((ROWS, B), BF), ((NZ, FL, B), BF)],
        "prep",
        [
            (SMEM, block_cols),
            (SMEM, block_count),
            (VMEM, x_t),
            (HBM, block_vals.reshape(K * B, B)),
        ],
        [pltpu.SemaphoreType.DMA],
    )
    with jax.named_scope("swap_vals"):
        peer = lax.ppermute(mine, "c", [(0, 1), (1, 0)])
    with jax.named_scope("gather_x"):
        a = lax.all_to_all(xb, "z", 0, 0, tiled=True)
        a = lax.all_to_all(jnp.broadcast_to(a, (NX, NZ, FL, B)), "x", 0, 0, tiled=True)
    parts, idx = call(
        agg_kernel,
        [((NC, FL, B), F32), ((NC, 8, B), jnp.int32)],
        "agg",
        [(VMEM, mine), (VMEM, peer), (VMEM, a)],
        [pltpu.SMEM((NC, 8, B), jnp.int32), pltpu.SemaphoreType.DMA],
    )
    with jax.named_scope("pair_agg"):
        parts = lax.all_gather(parts, "c", axis=0, tiled=False)
    ride = call(
        ride_kernel,
        ((NY, RIDE, B), BF),
        "ride",
        [(VMEM, parts), (VMEM, d_out_t), (VMEM, weight)],
    )
    with jax.named_scope("share_agg"):
        ride = lax.all_to_all(ride, "y", 0, 0, tiled=True)
    out_t, pack = call(mid_kernel, [((HL, B), BF), ((PACK, B), BF)], "mid", [(VMEM, ride)])
    with jax.named_scope("share_pair"):
        both = lax.all_gather(pack, "c", axis=0, tiled=False)
    term = call(
        back_kernel,
        ((NX, NZ * FL + FL, B), BF),
        "back",
        [(SMEM, idx), (VMEM, both), (VMEM, mine), (VMEM, peer)],
        [pltpu.VMEM((NX * NZ + 1, FL, B), F32)],
    )
    with jax.named_scope("scatter_x"):
        term = lax.all_to_all(term, "x", 0, 0, tiled=True)
    term = call(sum_kernel, ((NZ, 2 * FL, B), BF), "sum_x", [(VMEM, term)])
    with jax.named_scope("scatter_z"):
        term = lax.all_to_all(term, "z", 0, 0, tiled=True)
    half = call(half_kernel, ((FL, B), F32), "half", [(VMEM, term)])
    with jax.named_scope("join_w"):
        halves = lax.all_gather(half, "c", axis=0, tiled=False)
    grad_w, grad_x = call(
        last_kernel,
        [((FL, 2 * B), F32), ((FL, B), F32)],
        "last",
        [(VMEM, term), (VMEM, halves)],
    )
    return (out_t, grad_w, grad_x)


def solution(mesh):
    fine = Mesh(mesh.devices.reshape(NZ, NX, NC, NY), ("z", "x", "c", "y"))
    nodes = ("z", "x", "c")
    return jax.shard_map(
        local,
        mesh=fine,
        in_specs=(
            P("y", nodes),
            P("y", None),
            P(nodes, None),
            P(nodes),
            P(nodes, None, None, None),
            P("y", nodes),
        ),
        out_specs=(P("y", nodes), P("y", None), P("y", nodes)),
        check_vma=False,
    )
```

time: 118 us -> 105 us (0.89)
  blocking collectives: 86.9 us -> 56 us
  starting transfers between devices: 4.05 us -> 22.6 us
  waiting for transfers between devices: 0.75 us -> 16.1 us
  between operations: 14.7 us -> 1.36 us
  local copies, waits for them, and re-layouts: 5.18 us -> 3.28 us
  Pallas kernels: 4.06 us -> 5.68 us
  other arithmetic: 1.58 us -> 0 us
    all_to_all x2 -> x1, blocking collectives: 42.1 us -> 8.99 us  [local(): ride = lax.all_to_all(ride, 'y', 0, 0, tiled=True)]
    all_to_all x0 -> x1, starting transfers between devices: none -> 15.8 us  [local(): a = lax.all_to_all(xb, 'z', 0, 0, tiled=True)]
    all_to_all x0 -> x1, waiting for transfers between devices: none -> 9.13 us  [local(): a = lax.all_to_all(xb, 'z', 0, 0, tiled=True)]
    all_to_all x1, waiting for transfers between devices: 0.73 us -> 6.93 us  [local(): lax.all_to_all(jnp.broadcast_to(a, (NX, NZ, FL, B)), 'x', 0, 0, tiled=True)]
    ppermute x0 -> x1, starting transfers between devices: none -> 2.86 us  [local(): peer = lax.ppermute(mine, 'c', [(0, 1), (1, 0)])]
    pallas_call x4 -> x8, Pallas kernels: 4.06 us -> 5.68 us  [call(): pl.pallas_call(kernel, out_shape=shapes[0] if one else tuple(shapes), in_...]
    concatenate x1 -> x0, other arithmetic: 1.39 us -> none  [local(): jnp.concatenate([quarter, d_out_t, weight[:, :B], weight[:, B:]], axis=0)]
    slice x2 -> x0, local copies, waits for them, and re-layouts: 1.37 us -> none  [the longest x1 0.76 us: local(): weight[:, :B]]
  transfers between devices with their start and end apart: 2 -> 3, of which waited for: 1 -> 2; matrix products, arithmetic and copies ran while one was open for 1% -> 1% of each run, Pallas kernels for 0% -> 0%
where the time goes in v2:
time: 105 us
  blocking collectives  56 us (53%)
  starting transfers between devices  22.6 us (22%)
  waiting for transfers between devices  16.1 us (15%)
  Pallas kernels  5.68 us (5%)
  local copies, waits for them, and re-layouts  3.28 us (3%)
  between operations  1.36 us (1%)
    all_to_all x1, blocking collectives, local(): term = lax.all_to_all(term, 'z', 0, 0, tiled=True)  16.9 us
    all_to_all x1, starting transfers between devices, local(): a = lax.all_to_all(xb, 'z', 0, 0, tiled=True)  15.8 us
    all_to_all x1, blocking collectives, local(): term = lax.all_to_all(term, 'x', 0, 0, tiled=True)  11.8 us
    all_to_all x1, waiting for transfers between devices, local(): a = lax.all_to_all(xb, 'z', 0, 0, tiled=True)  9.13 us
    all_to_all x1, blocking collectives, local(): ride = lax.all_to_all(ride, 'y', 0, 0, tiled=True)  8.99 us
    all_gather x1, blocking collectives, local(): halves = lax.all_gather(half, 'c', axis=0, tiled=False)  8.32 us
    all_to_all x1, waiting for transfers between devices, local(): lax.all_to_all(jnp.broadcast_to(a, (NX, NZ, FL, B)), 'x', 0, 0, tiled=True)  6.93 us
    all_gather x1, blocking collectives, local(): parts = lax.all_gather(parts, 'c', axis=0, tiled=False)  6.59 us
  transfers between devices with their start and end apart: 3, of which 2 were waited for; matrix products, arithmetic and copies ran while one was open for 1% of the time, Pallas kernels for 0%

profile of v2, /device:TPU:1, one launch (start us, length us, event | category | flops | bytes accessed | tf_op | source)
XLA Modules:
  0.0 105.0 jit_solution(239070466514605528)
XLA Ops:
  1.3 0.0 copy-start.4
  1.3 0.6 copy-done.4
  1.9 0.0 copy-start
  1.9 1.0 copy-done
  3.0 0.0 copy-start.3
  3.0 0.7 copy-done.3
  3.7 1.3 %prep.1 = (bf16[2064,128]{1,0:T(8,128)(2,1)S(1)}, bf16[16,32,128]{2,1,0:T(8,128)(2,1)}) custom-call(s32[1,16]{1,0:T(1,128)S(1)} %copy-done.4, s32[1]{0:T(128)S(6)} %copy.9.count, bf16[32,128]{1,0:T(8,128)(2,1)S(1)} %copy-done.3, bf16[2048,128]{1,0:T(8,128)(2,1)S(1)} %bitcast.5), custom_call_target="tpu_custom_call" | custom-call | tf_op jit(solution)/shard_map/prep/pallas_call | solution.py:31
  4.9 15.8 %all-to-all-start = ((bf16[16,32,128]{2,1,0:T(8,128)(2,1)}), bf16[16,32,128]{2,1,0:T(8,128)(2,1)S(1)}, u32[]{:S(2)}, u32[]{:S(2)}) async-start(bf16[16,32,128]{2,1,0:T(8,128)(2,1)} %get-tuple-element.12), calls=%async_computation | async-start | bytes 262144 | tf_op jit(solution)/shard_map/gather_x/all_to_all | solution.py:165
  20.7 2.9 %collective-permute-start = (bf16[2064,128]{1,0:T(8,128)(2,1)S(1)}, bf16[2064,128]{1,0:T(8,128)(2,1)S(1)}, u32[]{:S(2)}, u32[]{:S(2)}) collective-permute-start(bf16[2064,128]{1,0:T(8,128)(2,1)S(1)} %get-tuple-element.11.mine), channel_id=1, source_target_pairs={{0,4},{4,0},{1,5},{5,1},{2,6},{6,2},{3,7},{7,3},{8,12},{12,8},{9,1... | collective-permute-start | bytes 1585160 | tf_op jit(solution)/shard_map/swap_vals/ppermute | solution.py:163
  23.6 9.1 %all-to-all-done = bf16[16,32,128]{2,1,0:T(8,128)(2,1)S(1)} async-done(((bf16[16,32,128]{2,1,0:T(8,128)(2,1)}), bf16[16,32,128]{2,1,0:T(8,128)(2,1)S(1)}, u32[]{:S(2)}, u32[]{:S(2)}) %all-to-all-start) | async-done | bytes 131104 | tf_op jit(solution)/shard_map/gather_x/all_to_all | solution.py:165
  32.7 0.9 broadcast_in_dim.3
  33.6 4.0 %all-to-all-start.1 = ((bf16[4,16,32,128]{3,2,1,0:T(8,128)(2,1)}), bf16[4,16,32,128]{3,2,1,0:T(8,128)(2,1)S(1)}, u32[]{:S(2)}, u32[]{:S(2)}) async-start(bf16[4,16,32,128]{3,2,1,0:T(8,128)(2,1)} %broadcast_in_dim.3), calls=%async_computation.1 | async-start | bytes 1048576 | tf_op jit(solution)/shard_map/gather_x/all_to_all | solution.py:166
  37.6 0.0 collective-permute-done.peer
  37.6 6.9 %all-to-all-done.1.xg = bf16[4,16,32,128]{3,2,1,0:T(8,128)(2,1)S(1)} async-done(((bf16[4,16,32,128]{3,2,1,0:T(8,128)(2,1)}), bf16[4,16,32,128]{3,2,1,0:T(8,128)(2,1)S(1)}, u32[]{:S(2)}, u32[]{:S(2)}) %all-to-all-start.1) | async-done | bytes 524320 | tf_op jit(solution)/shard_map/gather_x/all_to_all | solution.py:166
  44.5 1.3 %agg.1 = (f32[2,32,128]{2,1,0:T(8,128)S(1)}, s32[2,8,128]{2,1,0:T(8,128)S(1)}) custom-call(bf16[2064,128]{1,0:T(8,128)(2,1)S(1)} %get-tuple-element.11.mine, bf16[2064,128]{1,0:T(8,128)(2,1)S(1)} %collective-permute-done.peer, bf16[4,16,32,128]{3,2,1,0:T(8,128)(2,1)S(1)} %all-to-all-done.1.xg), custom_call_target="tpu_custom_call" | custom-call | tf_op jit(solution)/shard_map/agg/pallas_call | solution.py:31
  45.9 0.0 copy-start.1
  45.9 0.0 copy-start.2
  45.9 6.6 %all-gather = f32[4,32,128]{2,1,0:T(8,128)S(1)} all-gather(f32[2,32,128]{2,1,0:T(8,128)S(1)} %get-tuple-element.13), channel_id=2, replica_groups=mesh['z'=16,'x'=4,'c'=2,'y'=4] {'c'}, dimensions={0}, use_global_device_ids=true | all-gather | bytes 98304 | tf_op jit(solution)/shard_map/pair_agg/all_gather | solution.py:175
  52.5 0.0 copy-done.1
  52.5 0.0 copy-done.2
  52.5 9.0 %all_to_all.25.got = bf16[4,160,128]{2,1,0:T(8,128)(2,1)S(1)} all-to-all(bf16[4,160,128]{2,1,0:T(8,128)(2,1)S(1)} %ride.1), channel_id=1, replica_groups=mesh['z'=16,'x'=4,'c'=2,'y'=4] {'y'}, dimensions={0} | all-to-all | bytes 327680 | tf_op jit(solution)/shard_map/share_agg/all_to_all | solution.py:183
  61.5 1.0 mid.1
  62.5 3.3 %all-gather.1 = bf16[640,128]{1,0:T(8,128)(2,1)S(1)} all-gather(bf16[320,128]{1,0:T(8,128)(2,1)S(1)} %get-tuple-element.16), channel_id=3, replica_groups=mesh['z'=16,'x'=4,'c'=2,'y'=4] {'c'}, dimensions={0}, use_global_device_ids=true | all-gather | bytes 245760 | tf_op jit(solution)/shard_map/share_pair/all_gather | solution.py:186
  65.9 1.3 %back.1 = bf16[4,544,128]{2,1,0:T(8,128)(2,1)S(1)} custom-call(s32[2,8,128]{2,1,0:T(8,128)S(1)} %get-tuple-element.15.idx, bf16[2,320,128]{2,1,0:T(8,128)(2,1)S(1)} %bitcast.4, bf16[2064,128]{1,0:T(8,128)(2,1)S(1)} %get-tuple-element.11.mine, bf16[2064,128]{1,0:T(8,128)(2,1)S(1)} %collective-permute-done.peer), custom_call_target="tpu_custom_call" | custom-call | tf_op jit(solution)/shard_map/back/pallas_call | solution.py:31
  67.2 11.8 %all_to_all.26.got = bf16[4,544,128]{2,1,0:T(8,128)(2,1)S(1)} all-to-all(bf16[4,544,128]{2,1,0:T(8,128)(2,1)S(1)} %back.1), channel_id=1, replica_groups=mesh['z'=16,'x'=4,'c'=2,'y'=4] {'x'}, dimensions={0} | all-to-all | bytes 1114112 | tf_op jit(solution)/shard_map/scatter_x/all_to_all | solution.py:195
  79.0 0.1 sum_x.1
  79.0 16.9 %all_to_all.27.got = bf16[16,64,128]{2,1,0:T(8,128)(2,1)S(1)} all-to-all(bf16[16,64,128]{2,1,0:T(8,128)(2,1)S(1)} %sum_x.1), channel_id=1, replica_groups=mesh['z'=16,'x'=4,'c'=2,'y'=4] {'z'}, dimensions={0} | all-to-all | bytes 524288 | tf_op jit(solution)/shard_map/scatter_z/all_to_all | solution.py:198
  96.0 8.3 %all-gather.2 = f32[64,128]{1,0:T(8,128)S(1)} all-gather(f32[32,128]{1,0:T(8,128)S(1)} %half.1), channel_id=4, replica_groups=mesh['z'=16,'x'=4,'c'=2,'y'=4] {'c'}, dimensions={0}, use_global_device_ids=true | all-gather | bytes 49152 | tf_op jit(solution)/shard_map/join_w/all_gather | solution.py:201
  104.3 0.6 last.1
  (2 shorter events, 0.0 us)
Async XLA Ops:
  1.3 0.7 copy-start.4
  1.9 1.0 copy-start
  3.0 0.7 copy-start.3
  4.9 27.8 %all-to-all-start = ((bf16[16,32,128]{2,1,0:T(8,128)(2,1)}), bf16[16,32,128]{2,1,0:T(8,128)(2,1)S(1)}, u32[]{:S(2)}, u32[]{:S(2)}) async-start(bf16[16,32,128]{2,1,0:T(8,128)(2,1)} %get-tuple-element.12), calls=%async_computation | async-start | bytes 262144 | tf_op jit(solution)/shard_map/gather_x/all_to_all | solution.py:165
  20.7 16.9 %collective-permute-start = (bf16[2064,128]{1,0:T(8,128)(2,1)S(1)}, bf16[2064,128]{1,0:T(8,128)(2,1)S(1)}, u32[]{:S(2)}, u32[]{:S(2)}) collective-permute-start(bf16[2064,128]{1,0:T(8,128)(2,1)S(1)} %get-tuple-element.11.mine), channel_id=1, source_target_pairs={{0,4},{4,0},{1,5},{5,1},{2,6},{6,2},{3,7},{7,3},{8,12},{12,8},{9,1... | collective-permute-start | bytes 1585160 | tf_op jit(solution)/shard_map/swap_vals/ppermute | solution.py:163
  33.6 10.9 %all-to-all-start.1 = ((bf16[4,16,32,128]{3,2,1,0:T(8,128)(2,1)}), bf16[4,16,32,128]{3,2,1,0:T(8,128)(2,1)S(1)}, u32[]{:S(2)}, u32[]{:S(2)}) async-start(bf16[4,16,32,128]{3,2,1,0:T(8,128)(2,1)} %broadcast_in_dim.3), calls=%async_computation.1 | async-start | bytes 1048576 | tf_op jit(solution)/shard_map/gather_x/all_to_all | solution.py:166
  45.9 6.6 %copy-start.1 = (bf16[64,128]{1,0:T(8,128)(2,1)S(1)}, bf16[64,128]{1,0:T(8,128)(2,1)}, u32[]{:S(2)}) copy-start(bf16[64,128]{1,0:T(8,128)(2,1)} %d_out.1) | copy-start | bytes 49156
  45.9 6.6 %copy-start.2 = (bf16[32,256]{1,0:T(8,128)(2,1)S(1)}, bf16[32,256]{1,0:T(8,128)(2,1)}, u32[]{:S(2)}) copy-start(bf16[32,256]{1,0:T(8,128)(2,1)} %weight.1) | copy-start | bytes 49156

commit v3 on v2

v3 whole, which is shorter than its diff:
```python
import jax
import jax.numpy as jnp
from jax import lax
from jax.experimental import pallas as pl
from jax.experimental.pallas import tpu as pltpu
from jax.sharding import Mesh, PartitionSpec as P

BF = jnp.bfloat16
F32 = jnp.float32
NZ, NX, NC, NY = 16, 4, 2, 4
K, B, FL, HL = 16, 128, 32, 64
SMALL = HL + 16
RIDE = NC * FL + NC * HL + 2 * FL
D_AT, W_AT = NC * FL, NC * FL + NC * HL
C0, C1 = 0.7978845608, 0.044715
VM = pltpu.CompilerParams(vmem_limit_bytes=32 * 1024 * 1024)
VMEM = pl.BlockSpec(memory_space=pltpu.VMEM)
SMEM = pl.BlockSpec(memory_space=pltpu.SMEM)


def dot(a, b, ca, cb):
    return lax.dot_general(a, b, (((ca,), (cb,)), ((), ())), preferred_element_type=F32)


def call(kernel, outs, name, ins, scratch=()):
    specs, args = zip(*ins)
    one = not isinstance(outs, list)
    shapes = [jax.ShapeDtypeStruct(*o) for o in ((outs,) if one else outs)]
    return pl.pallas_call(
        kernel,
        out_shape=shapes[0] if one else tuple(shapes),
        in_specs=list(specs),
        out_specs=VMEM if one else tuple(VMEM for _ in shapes),
        scratch_shapes=list(scratch),
        compiler_params=VM,
        name=name,
    )(*args)


def small_kernel(cols, count, d_out, out):
    lane = lax.broadcasted_iota(jnp.int32, (16, B), 1)
    meta = jnp.where(lane == K, count[0], 0)
    for s in range(K):
        meta = jnp.where(lane == s, cols[0, s], meta)
    out[0:HL, :] = d_out[...]
    out[HL:, :] = meta.astype(F32).astype(BF)


def agg_kernel(small, other, mine, peer, xg, out, idx, ints, sem):
    core = lax.axis_index("c")
    for r, got in enumerate((small, other)):
        idx[r] = got[HL:, :].astype(F32)[0:8].astype(jnp.int32)
    copy = pltpu.make_async_copy(idx, ints, sem)
    copy.start()
    copy.wait()
    for r, blocks in enumerate((mine, peer)):
        acc = jnp.zeros((FL, B), F32)
        for s in range(K):
            owner = ints[r, 0, s]
            use = jnp.logical_and(owner % NC == core, s < ints[r, 0, K])
            got = xg[(owner // NC) % NX, owner // (NC * NX)]
            got = jnp.where(use, got, jnp.zeros_like(got))
            acc = acc + dot(got, blocks[s * B : (s + 1) * B, :], 1, 1)
        out[r] = acc


def ride_kernel(parts, small, other, weight, out):
    core = lax.axis_index("c")
    for y in range(NY):
        out[y, W_AT : W_AT + FL, :] = weight[:, :B]
        out[y, W_AT + FL :, :] = weight[:, B:]
    for c in range(NC):
        agg = (parts[c, 0] + parts[1 - c, 1]).astype(BF)
        cot = jnp.where(core == c, small[0:HL, :].astype(F32), other[0:HL, :].astype(F32))
        for y in range(NY):
            out[y, c * FL : (c + 1) * FL, :] = agg
            out[y, D_AT + c * HL : D_AT + (c + 1) * HL, :] = cot.astype(BF)


def back_kernel(idx, got, mine, peer, out_t, out, term, hidden):
    core, y_at = lax.axis_index("c"), lax.axis_index("y")
    term[...] = jnp.zeros_like(term)
    agg = jnp.concatenate(
        [
            jnp.concatenate([got[y, c * FL : (c + 1) * FL, :] for y in range(NY)], axis=0)
            for c in range(NC)
        ],
        axis=1,
    )
    own = jnp.concatenate([got[y_at, c * FL : (c + 1) * FL, :] for c in range(NC)], axis=1)
    back = jnp.zeros((FL, NC * B), F32)
    for h in range(2):
        rows = slice(W_AT + h * FL, W_AT + (h + 1) * FL)
        w = jnp.concatenate([got[y, rows, :] for y in range(NY)], axis=0)
        pre = dot(w, agg, 0, 0)
        t = jnp.tanh(C0 * (pre + C1 * (pre * pre * pre)))
        val = (0.5 * pre * (1.0 + t)).astype(BF)
        der = 0.5 * (1.0 + t) + 0.5 * pre * (1.0 - t * t) * (C0 * (1.0 + 3.0 * C1 * (pre * pre)))
        for c in range(NC):
            for q in range(2):

                @pl.when(jnp.logical_and(core == c, y_at == 2 * h + q))
                def _():
                    out_t[...] = val[q * HL : (q + 1) * HL, c * B : (c + 1) * B]

        cot = jnp.concatenate(
            [
                jnp.concatenate(
                    [got[2 * h + q, D_AT + c * HL : D_AT + (c + 1) * HL, :] for q in range(2)],
                    axis=0,
                )
                for c in range(NC)
            ],
            axis=1,
        )
        grad = (cot.astype(F32) * der).astype(BF)
        hidden[h] = grad
        back = back + dot(got[y_at, rows, :], grad, 1, 0)
    gw = dot(own, hidden[core], 1, 1).astype(BF)
    back = back.astype(BF)
    for r, blocks in enumerate((mine, peer)):
        mix = back[:, :B], back[:, B:]
        first = core == 0 if r == 0 else core == 1
        grad = jnp.where(first, mix[0], mix[1])
        for s in range(K):
            owner = idx[r, 0, s]
            use = jnp.logical_and(owner % NC == core, s < idx[r, 0, K])
            at = ((owner // NC) % NX) * NZ + owner // (NC * NX)
            at = jnp.where(use, at, NX * NZ)
            term[at] = term[at] + dot(grad, blocks[s * B : (s + 1) * B, :], 1, 0)
    for x in range(NX):
        for z in range(NZ):
            out[x, z * FL : (z + 1) * FL, :] = term[x * NZ + z].astype(BF)
        out[x, NZ * FL :, :] = gw


def sum_kernel(got, out):
    gw = sum(got[x, NZ * FL :, :].astype(F32) for x in range(NX)).astype(BF)
    for z in range(NZ):
        rows = slice(z * FL, (z + 1) * FL)
        out[z, 0:FL, :] = sum(got[x, rows, :].astype(F32) for x in range(NX)).astype(BF)
        out[z, FL:, :] = gw


def half_kernel(got, out):
    out[...] = sum(got[z, FL:, :].astype(F32) for z in range(NZ))


def last_kernel(got, halves, grad_w, grad_x):
    grad_w[:, :B] = halves[0]
    grad_w[:, B:] = halves[1]
    grad_x[...] = sum(got[z, 0:FL, :].astype(F32) for z in range(NZ))


def local(x_t, weight, block_cols, block_count, block_vals, d_out_t):
    mine = block_vals.reshape(K * B, B)
    with jax.named_scope("gather_x"):
        a = lax.all_to_all(jnp.broadcast_to(x_t, (NZ, FL, B)), "z", 0, 0, tiled=True)
    small = call(
        small_kernel,
        ((SMALL, B), BF),
        "small",
        [(SMEM, block_cols), (SMEM, block_count), (VMEM, d_out_t)],
    )
    with jax.named_scope("swap_core"):
        peer = lax.ppermute(mine, "c", [(0, 1), (1, 0)])
        other = lax.ppermute(small, "c", [(0, 1), (1, 0)])
    with jax.named_scope("gather_x"):
        a = lax.all_to_all(jnp.broadcast_to(a, (NX, NZ, FL, B)), "x", 0, 0, tiled=True)
    parts, idx = call(
        agg_kernel,
        [((NC, FL, B), F32), ((NC, 8, B), jnp.int32)],
        "agg",
        [(VMEM, small), (VMEM, other), (VMEM, mine), (VMEM, peer), (VMEM, a)],
        [pltpu.SMEM((NC, 8, B), jnp.int32), pltpu.SemaphoreType.DMA],
    )
    with jax.named_scope("pair_agg"):
        parts = lax.all_gather(parts, "c", axis=0, tiled=False)
    ride = call(
        ride_kernel,
        ((NY, RIDE, B), BF),
        "ride",
        [(VMEM, parts), (VMEM, small), (VMEM, other), (VMEM, weight)],
    )
    with jax.named_scope("share_agg"):
        ride = lax.all_to_all(ride, "y", 0, 0, tiled=True)
    out_t, term = call(
        back_kernel,
        [((HL, B), BF), ((NX, NZ * FL + FL, B), BF)],
        "back",
        [(SMEM, idx), (VMEM, ride), (VMEM, mine), (VMEM, peer)],
        [pltpu.VMEM((NX * NZ + 1, FL, B), F32), pltpu.VMEM((2, B, NC * B), BF)],
    )
    with jax.named_scope("scatter_x"):
        term = lax.all_to_all(term, "x", 0, 0, tiled=True)
    term = call(sum_kernel, ((NZ, 2 * FL, B), BF), "sum_x", [(VMEM, term)])
    with jax.named_scope("scatter_z"):
        term = lax.all_to_all(term, "z", 0, 0, tiled=True)
    half = call(half_kernel, ((FL, B), F32), "half", [(VMEM, term)])
    with jax.named_scope("join_w"):
        halves = lax.all_gather(half, "c", axis=0, tiled=False)
    grad_w, grad_x = call(
        last_kernel,
        [((FL, 2 * B), F32), ((FL, B), F32)],
        "last",
        [(VMEM, term), (VMEM, halves)],
    )
    return (out_t, grad_w, grad_x)


def solution(mesh):
    fine = Mesh(mesh.devices.reshape(NZ, NX, NC, NY), ("z", "x", "c", "y"))
    nodes = ("z", "x", "c")
    return jax.shard_map(
        local,
        mesh=fine,
        in_specs=(
            P("y", nodes),
            P("y", None),
            P(nodes, None),
            P(nodes),
            P(nodes, None, None, None),
            P("y", nodes),
        ),
        out_specs=(P("y", nodes), P("y", None), P("y", nodes)),
        check_vma=False,
    )
```

time: 105 us -> 98.7 us (0.940)
  waiting for transfers between devices: 16.1 us -> 9.95 us
  starting transfers between devices: 22.6 us -> 28.6 us
  blocking collectives: 56 us -> 51 us
    all_to_all x1, waiting for transfers between devices: 6.93 us -> 0.01 us  [local(): lax.all_to_all(jnp.broadcast_to(a, (NX, NZ, FL, B)), 'x', 0, 0, tiled=True)]
    ppermute x0 -> x1, starting transfers between devices: none -> 5.84 us  [local(): other = lax.ppermute(small, 'c', [(0, 1), (1, 0)])]
    all_gather x1 -> x0, blocking collectives: 3.33 us -> none  [local(): both = lax.all_gather(pack, 'c', axis=0, tiled=False)]
    unnamed x10 -> x8, local copies, waits for them, and re-layouts: 2.4 us -> 0.02 us
    broadcast_in_dim x0 -> x1, local copies, waits for them, and re-layouts: none -> 1.36 us  [local(): jnp.broadcast_to(x_t, (NZ, FL, B))]
    all_to_all x1, blocking collectives: 11.8 us -> 10.4 us  [local(): term = lax.all_to_all(term, 'x', 0, 0, tiled=True)]
    pallas_call x8 -> x7, Pallas kernels: 5.68 us -> 5.01 us  [call(): pl.pallas_call(kernel, out_shape=shapes[0] if one else tuple(shapes), in_...]
  transfers between devices with their start and end apart: 3 -> 4, of which waited for: 2 -> 2; matrix products, arithmetic and copies ran while one was open for 1% -> 1% of each run, Pallas kernels for 0% -> 1%
where the time goes in v3:
time: 98.7 us; the launch traced here: 98.2 us
  blocking collectives  51 us (52%)
  starting transfers between devices  28.6 us (29%)
  waiting for transfers between devices  9.95 us (10%)
  Pallas kernels  5.01 us (5%)
  local copies, waits for them, and re-layouts  2.27 us (2%)
  between operations  1.38 us (1%)
    all_to_all x1, blocking collectives, local(): term = lax.all_to_all(term, 'z', 0, 0, tiled=True)  16.9 us
    all_to_all x1, starting transfers between devices, local(): lax.all_to_all(jnp.broadcast_to(x_t, (NZ, FL, B)), 'z', 0, 0, tiled=True)  15.7 us
    all_to_all x1, blocking collectives, local(): term = lax.all_to_all(term, 'x', 0, 0, tiled=True)  10.4 us
    all_to_all x1, blocking collectives, local(): ride = lax.all_to_all(ride, 'y', 0, 0, tiled=True)  9.82 us
    all_to_all x1, waiting for transfers between devices, local(): lax.all_to_all(jnp.broadcast_to(x_t, (NZ, FL, B)), 'z', 0, 0, tiled=True)  9.12 us
    all_gather x1, blocking collectives, local(): halves = lax.all_gather(half, 'c', axis=0, tiled=False)  8.19 us
    ppermute x1, starting transfers between devices, local(): other = lax.ppermute(small, 'c', [(0, 1), (1, 0)])  5.84 us
    all_gather x1, blocking collectives, local(): parts = lax.all_gather(parts, 'c', axis=0, tiled=False)  5.59 us
  transfers between devices with their start and end apart: 4, of which 2 were waited for; matrix products, arithmetic and copies ran while one was open for 1% of the time, Pallas kernels for 1%

profile of v3, /device:TPU:1, one launch (start us, length us, event | category | flops | bytes accessed | tf_op | source)
XLA Modules:
  0.0 98.2 jit_solution(299732231176693802)
XLA Ops:
  0.6 1.4 %broadcast_in_dim.6 = bf16[16,32,128]{2,1,0:T(8,128)(2,1)} broadcast(bf16[32,128]{1,0:T(8,128)(2,1)} %param.6), dimensions={1,2} | broadcast | bytes 139264 | tf_op jit(solution)/shard_map/gather_x/broadcast_in_dim | solution.py:158
  2.0 15.7 %all-to-all-start = ((bf16[16,32,128]{2,1,0:T(8,128)(2,1)}), bf16[16,32,128]{2,1,0:T(8,128)(2,1)S(1)}, u32[]{:S(2)}, u32[]{:S(2)}) async-start(bf16[16,32,128]{2,1,0:T(8,128)(2,1)} %broadcast_in_dim.6), calls=%async_computation | async-start | bytes 262144 | tf_op jit(solution)/shard_map/gather_x/all_to_all | solution.py:158
  17.7 2.9 %collective-permute-start.1 = (bf16[2048,128]{1,0:T(8,128)(2,1)}, bf16[2048,128]{1,0:T(8,128)(2,1)S(1)}, u32[]{:S(2)}, u32[]{:S(2)}) collective-permute-start(bf16[2048,128]{1,0:T(8,128)(2,1)} %bitcast.3), channel_id=1, source_target_pairs={{0,4},{4,0},{1,5},{5,1},{2,6},{6,2},{3,7},{7,3},{8,12},{12,8},{9,1... | collective-permute-start | bytes 1572872 | tf_op jit(solution)/shard_map/swap_core/ppermute | solution.py:166
  20.6 9.1 %all-to-all-done = bf16[16,32,128]{2,1,0:T(8,128)(2,1)S(1)} async-done(((bf16[16,32,128]{2,1,0:T(8,128)(2,1)}), bf16[16,32,128]{2,1,0:T(8,128)(2,1)S(1)}, u32[]{:S(2)}, u32[]{:S(2)}) %all-to-all-start) | async-done | bytes 131104 | tf_op jit(solution)/shard_map/gather_x/all_to_all | solution.py:158
  29.7 0.9 broadcast_in_dim.7
  30.6 0.0 copy-start.2
  30.6 0.0 copy-start
  30.6 4.1 %all-to-all-start.1 = ((bf16[4,16,32,128]{3,2,1,0:T(8,128)(2,1)}), bf16[4,16,32,128]{3,2,1,0:T(8,128)(2,1)S(1)}, u32[]{:S(2)}, u32[]{:S(2)}) async-start(bf16[4,16,32,128]{3,2,1,0:T(8,128)(2,1)} %broadcast_in_dim.7), calls=%async_computation.1 | async-start | bytes 1048576 | tf_op jit(solution)/shard_map/gather_x/all_to_all | solution.py:169
  34.8 0.0 copy-start.3
  35.4 0.0 copy-done.2
  35.5 0.0 copy-done.3
  35.5 0.6 small.1
  36.0 5.8 %collective-permute-start = (bf16[80,128]{1,0:T(8,128)(2,1)S(1)}, bf16[80,128]{1,0:T(8,128)(2,1)S(1)}, u32[]{:S(2)}, u32[]{:S(2)}) collective-permute-start(bf16[80,128]{1,0:T(8,128)(2,1)S(1)} %small.1), channel_id=1, source_target_pairs={{0,4},{4,0},{1,5},{5,1},{2,6},{6,2},{3,7},{7,3},{8,12},{12,8},{9,1... | collective-permute-start | bytes 61448 | tf_op jit(solution)/shard_map/swap_core/ppermute | solution.py:167
  41.9 0.8 collective-permute-done.other
  42.7 0.0 collective-permute-done.1.peer
  42.7 0.0 all-to-all-done.1.xg
  42.7 0.0 copy-done
  42.7 1.3 %agg.1 = (f32[2,32,128]{2,1,0:T(8,128)S(1)}, s32[2,8,128]{2,1,0:T(8,128)S(1)}) custom-call(bf16[80,128]{1,0:T(8,128)(2,1)S(1)} %small.1, bf16[80,128]{1,0:T(8,128)(2,1)S(1)} %collective-permute-done.other, bf16[2048,128]{1,0:T(8,128)(2,1)S(1)} %bitcast.4, bf16[2048,128]{1,0:T(8,128)(2,1)S(1)} %collective-permute-done.1.peer, ...), custom_call_target="tpu_custom_call" | custom-call | tf_op jit(solution)/shard_map/agg/pallas_call | solution.py:29
  44.1 0.0 copy-start.1
  44.1 5.6 %all-gather = f32[4,32,128]{2,1,0:T(8,128)S(1)} all-gather(f32[2,32,128]{2,1,0:T(8,128)S(1)} %get-tuple-element.10), channel_id=2, replica_groups=mesh['z'=16,'x'=4,'c'=2,'y'=4] {'c'}, dimensions={0}, use_global_device_ids=true | all-gather | bytes 98304 | tf_op jit(solution)/shard_map/pair_agg/all_gather | solution.py:178
  49.7 0.0 copy-done.1
  49.7 9.8 %all_to_all.25.got = bf16[4,256,128]{2,1,0:T(8,128)(2,1)S(1)} all-to-all(bf16[4,256,128]{2,1,0:T(8,128)(2,1)S(1)} %ride.1), channel_id=1, replica_groups=mesh['z'=16,'x'=4,'c'=2,'y'=4] {'y'}, dimensions={0} | all-to-all | bytes 524288 | tf_op jit(solution)/shard_map/share_agg/all_to_all | solution.py:186
  59.5 2.4 %back.1 = (bf16[64,128]{1,0:T(8,128)(2,1)}, bf16[4,544,128]{2,1,0:T(8,128)(2,1)S(1)}) custom-call(s32[2,8,128]{2,1,0:T(8,128)S(1)} %get-tuple-element.9.idx, bf16[4,256,128]{2,1,0:T(8,128)(2,1)S(1)} %all_to_all.25.got, bf16[2048,128]{1,0:T(8,128)(2,1)S(1)} %bitcast.5, bf16[2048,128]{1,0:T(8,128)(2,1)S(1)} %collective-permute-done.1.peer), custom_call_target="tpu_custom_call" | custom-call | tf_op jit(solution)/shard_map/back/pallas_call | solution.py:29
  61.9 10.4 %all_to_all.26.got = bf16[4,544,128]{2,1,0:T(8,128)(2,1)S(1)} all-to-all(bf16[4,544,128]{2,1,0:T(8,128)(2,1)S(1)} %get-tuple-element.12), channel_id=1, replica_groups=mesh['z'=16,'x'=4,'c'=2,'y'=4] {'x'}, dimensions={0} | all-to-all | bytes 1114112 | tf_op jit(solution)/shard_map/scatter_x/all_to_all | solution.py:195
  72.3 0.1 sum_x.1
  72.4 16.9 %all_to_all.27.got = bf16[16,64,128]{2,1,0:T(8,128)(2,1)S(1)} all-to-all(bf16[16,64,128]{2,1,0:T(8,128)(2,1)S(1)} %sum_x.1), channel_id=1, replica_groups=mesh['z'=16,'x'=4,'c'=2,'y'=4] {'z'}, dimensions={0} | all-to-all | bytes 524288 | tf_op jit(solution)/shard_map/scatter_z/all_to_all | solution.py:198
  89.3 8.2 %all-gather.1 = f32[64,128]{1,0:T(8,128)S(1)} all-gather(f32[32,128]{1,0:T(8,128)S(1)} %half.1), channel_id=3, replica_groups=mesh['z'=16,'x'=4,'c'=2,'y'=4] {'c'}, dimensions={0}, use_global_device_ids=true | all-gather | bytes 49152 | tf_op jit(solution)/shard_map/join_w/all_gather | solution.py:201
  97.5 0.6 last.1
  (2 shorter events, 0.1 us)
Async XLA Ops:
  2.0 27.8 %all-to-all-start = ((bf16[16,32,128]{2,1,0:T(8,128)(2,1)}), bf16[16,32,128]{2,1,0:T(8,128)(2,1)S(1)}, u32[]{:S(2)}, u32[]{:S(2)}) async-start(bf16[16,32,128]{2,1,0:T(8,128)(2,1)} %broadcast_in_dim.6), calls=%async_computation | async-start | bytes 262144 | tf_op jit(solution)/shard_map/gather_x/all_to_all | solution.py:158
  17.7 25.0 %collective-permute-start.1 = (bf16[2048,128]{1,0:T(8,128)(2,1)}, bf16[2048,128]{1,0:T(8,128)(2,1)S(1)}, u32[]{:S(2)}, u32[]{:S(2)}) collective-permute-start(bf16[2048,128]{1,0:T(8,128)(2,1)} %bitcast.3), channel_id=1, source_target_pairs={{0,4},{4,0},{1,5},{5,1},{2,6},{6,2},{3,7},{7,3},{8,12},{12,8},{9,1... | collective-permute-start | bytes 1572872 | tf_op jit(solution)/shard_map/swap_core/ppermute | solution.py:166
  30.6 4.8 %copy-start.2 = (bf16[64,128]{1,0:T(8,128)(2,1)S(1)}, bf16[64,128]{1,0:T(8,128)(2,1)}, u32[]{:S(2)}) copy-start(bf16[64,128]{1,0:T(8,128)(2,1)} %d_out.1) | copy-start | bytes 49156
  30.6 12.1 %copy-start = (bf16[1,16,128,128]{3,2,1,0:T(8,128)(2,1)S(1)}, bf16[1,16,128,128]{3,2,1,0:T(8,128)(2,1)}, u32[]{:S(2)}) copy-start(bf16[1,16,128,128]{3,2,1,0:T(8,128)(2,1)} %param.10) | copy-start | bytes 1572868
  30.6 12.1 %all-to-all-start.1 = ((bf16[4,16,32,128]{3,2,1,0:T(8,128)(2,1)}), bf16[4,16,32,128]{3,2,1,0:T(8,128)(2,1)S(1)}, u32[]{:S(2)}, u32[]{:S(2)}) async-start(bf16[4,16,32,128]{3,2,1,0:T(8,128)(2,1)} %broadcast_in_dim.7), calls=%async_computation.1 | async-start | bytes 1048576 | tf_op jit(solution)/shard_map/gather_x/all_to_all | solution.py:169
  34.8 0.7 copy-start.3
  36.0 6.7 %collective-permute-start = (bf16[80,128]{1,0:T(8,128)(2,1)S(1)}, bf16[80,128]{1,0:T(8,128)(2,1)S(1)}, u32[]{:S(2)}, u32[]{:S(2)}) collective-permute-start(bf16[80,128]{1,0:T(8,128)(2,1)S(1)} %small.1), channel_id=1, source_target_pairs={{0,4},{4,0},{1,5},{5,1},{2,6},{6,2},{3,7},{7,3},{8,12},{12,8},{9,1... | collective-permute-start | bytes 61448 | tf_op jit(solution)/shard_map/swap_core/ppermute | solution.py:167
  44.1 5.6 %copy-start.1 = (bf16[32,256]{1,0:T(8,128)(2,1)S(1)}, bf16[32,256]{1,0:T(8,128)(2,1)}, u32[]{:S(2)}) copy-start(bf16[32,256]{1,0:T(8,128)(2,1)} %weight.1) | copy-start | bytes 49156

commit v4 on v3

--- a/solution.py
+++ b/solution.py
@@ -7,7 +7,8 @@
 
 BF = jnp.bfloat16
 F32 = jnp.float32
-NZ, NX, NC, NY = 16, 4, 2, 4
+NZ, NW, NX, NC, NY = 8, 2, 4, 2, 4
+NP = NW * NX
 K, B, FL, HL = 16, 128, 32, 64
 SMALL = HL + 16
 RIDE = NC * FL + NC * HL + 2 * FL
@@ -58,7 +59,7 @@
         for s in range(K):
             owner = ints[r, 0, s]
             use = jnp.logical_and(owner % NC == core, s < ints[r, 0, K])
-            got = xg[(owner // NC) % NX, owner // (NC * NX)]
+            got = xg[(owner // NC) % NP, owner // (NC * NP)]
             got = jnp.where(use, got, jnp.zeros_like(got))
             acc = acc + dot(got, blocks[s * B : (s + 1) * B, :], 1, 1)
         out[r] = acc
@@ -125,20 +126,20 @@
         for s in range(K):
             owner = idx[r, 0, s]
             use = jnp.logical_and(owner % NC == core, s < idx[r, 0, K])
-            at = ((owner // NC) % NX) * NZ + owner // (NC * NX)
-            at = jnp.where(use, at, NX * NZ)
+            at = ((owner // NC) % NP) * NZ + owner // (NC * NP)
+            at = jnp.where(use, at, NP * NZ)
             term[at] = term[at] + dot(grad, blocks[s * B : (s + 1) * B, :], 1, 0)
-    for x in range(NX):
+    for x in range(NP):
         for z in range(NZ):
             out[x, z * FL : (z + 1) * FL, :] = term[x * NZ + z].astype(BF)
         out[x, NZ * FL :, :] = gw
 
 
 def sum_kernel(got, out):
-    gw = sum(got[x, NZ * FL :, :].astype(F32) for x in range(NX)).astype(BF)
+    gw = sum(got[x, NZ * FL :, :].astype(F32) for x in range(NP)).astype(BF)
     for z in range(NZ):
         rows = slice(z * FL, (z + 1) * FL)
-        out[z, 0:FL, :] = sum(got[x, rows, :].astype(F32) for x in range(NX)).astype(BF)
+        out[z, 0:FL, :] = sum(got[x, rows, :].astype(F32) for x in range(NP)).astype(BF)
         out[z, FL:, :] = gw
 
 
@@ -166,7 +167,7 @@
         peer = lax.ppermute(mine, "c", [(0, 1), (1, 0)])
         other = lax.ppermute(small, "c", [(0, 1), (1, 0)])
     with jax.named_scope("gather_x"):
-        a = lax.all_to_all(jnp.broadcast_to(a, (NX, NZ, FL, B)), "x", 0, 0, tiled=True)
+        a = lax.all_to_all(jnp.broadcast_to(a, (NP, NZ, FL, B)), ("w", "x"), 0, 0, tiled=True)
     parts, idx = call(
         agg_kernel,
         [((NC, FL, B), F32), ((NC, 8, B), jnp.int32)],
@@ -186,13 +187,13 @@
         ride = lax.all_to_all(ride, "y", 0, 0, tiled=True)
     out_t, term = call(
         back_kernel,
-        [((HL, B), BF), ((NX, NZ * FL + FL, B), BF)],
+        [((HL, B), BF), ((NP, NZ * FL + FL, B), BF)],
         "back",
         [(SMEM, idx), (VMEM, ride), (VMEM, mine), (VMEM, peer)],
-        [pltpu.VMEM((NX * NZ + 1, FL, B), F32), pltpu.VMEM((2, B, NC * B), BF)],
+        [pltpu.VMEM((NP * NZ + 1, FL, B), F32), pltpu.VMEM((2, B, NC * B), BF)],
     )
     with jax.named_scope("scatter_x"):
-        term = lax.all_to_all(term, "x", 0, 0, tiled=True)
+        term = lax.all_to_all(term, ("w", "x"), 0, 0, tiled=True)
     term = call(sum_kernel, ((NZ, 2 * FL, B), BF), "sum_x", [(VMEM, term)])
     with jax.named_scope("scatter_z"):
         term = lax.all_to_all(term, "z", 0, 0, tiled=True)
@@ -209,8 +210,8 @@
 
 
 def solution(mesh):
-    fine = Mesh(mesh.devices.reshape(NZ, NX, NC, NY), ("z", "x", "c", "y"))
-    nodes = ("z", "x", "c")
+    fine = Mesh(mesh.devices.reshape(NZ, NW, NX, NC, NY), ("z", "w", "x", "c", "y"))
+    nodes = ("z", "w", "x", "c")
     return jax.shard_map(
         local,
         mesh=fine,

time: 98.7 us -> 95.6 us (0.969)
  blocking collectives: 51 us -> 74.9 us
  starting transfers between devices: 28.6 us -> 11.1 us
  waiting for transfers between devices: 9.95 us -> 1.16 us
    all_to_all x1 -> x2, blocking collectives: 10.4 us -> 40.9 us  [the longest x1 27.6 us: local(): lax.all_to_all(jnp.broadcast_to(x_t, (NZ, FL, B)), 'z', 0, 0, tiled=True)]
    all_to_all x2 -> x1, starting transfers between devices: 19.9 us -> 4.26 us  [local(): lax.all_to_all(jnp.broadcast_to(a, (NP, NZ, FL, B)), ('w', 'x'), 0, 0, ti...]
    all_to_all x2 -> x1, waiting for transfers between devices: 9.13 us -> 0.01 us  [local(): lax.all_to_all(jnp.broadcast_to(a, (NP, NZ, FL, B)), ('w', 'x'), 0, 0, ti...]
    ppermute x1, starting transfers between devices: 5.84 us -> 1.92 us  [local(): other = lax.ppermute(small, 'c', [(0, 1), (1, 0)])]
    all_gather x1, blocking collectives: 8.19 us -> 5.19 us  [local(): halves = lax.all_gather(half, 'c', axis=0, tiled=False)]
    all_gather x1, blocking collectives: 5.59 us -> 3.53 us  [local(): parts = lax.all_gather(parts, 'c', axis=0, tiled=False)]
    ppermute x1, starting transfers between devices: 2.87 us -> 4.89 us  [local(): peer = lax.ppermute(mine, 'c', [(0, 1), (1, 0)])]
    all_to_all x1, blocking collectives: 16.9 us -> 15.5 us  [local(): term = lax.all_to_all(term, 'z', 0, 0, tiled=True)]
  transfers between devices with their start and end apart: 4 -> 3, of which waited for: 2 -> 1; matrix products, arithmetic and copies ran while one was open for 1% -> 0% of each run, Pallas kernels for 1% -> 1%
where the time goes in v4:
time: 95.6 us; the launch traced here: 95.1 us
  blocking collectives  74.9 us (78%)
  starting transfers between devices  11.1 us (12%)
  Pallas kernels  5 us (5%)
  local copies, waits for them, and re-layouts  1.61 us (2%)
  between operations  1.36 us (1%)
  waiting for transfers between devices  1.16 us (1%)
    all_to_all x1, blocking collectives, local(): lax.all_to_all(jnp.broadcast_to(x_t, (NZ, FL, B)), 'z', 0, 0, tiled=True)  27.6 us
    all_to_all x1, blocking collectives, local(): term = lax.all_to_all(term, 'z', 0, 0, tiled=True)  15.5 us
    all_to_all x1, blocking collectives, local(): term = lax.all_to_all(term, ('w', 'x'), 0, 0, tiled=True)  13.2 us
    all_to_all x1, blocking collectives, local(): ride = lax.all_to_all(ride, 'y', 0, 0, tiled=True)  9.82 us
    all_gather x1, blocking collectives, local(): halves = lax.all_gather(half, 'c', axis=0, tiled=False)  5.19 us
    pallas_call x7, Pallas kernels, call(): pl.pallas_call(kernel, out_shape=shapes[0] if one else tuple(shapes), in_...  5 us
    ppermute x1, starting transfers between devices, local(): peer = lax.ppermute(mine, 'c', [(0, 1), (1, 0)])  4.89 us
    all_to_all x1, starting transfers between devices, local(): lax.all_to_all(jnp.broadcast_to(a, (NP, NZ, FL, B)), ('w', 'x'), 0, 0, ti...  4.26 us
  transfers between devices with their start and end apart: 3, of which 1 were waited for; matrix products, arithmetic and copies ran while one was open for 0% of the time, Pallas kernels for 1%

profile of v4, /device:TPU:1, one launch (start us, length us, event | category | flops | bytes accessed | tf_op | source)
XLA Modules:
  0.0 95.1 jit_solution(17227387588215947072)
XLA Ops:
  0.6 0.7 broadcast_in_dim.6
  1.3 27.6 %all_to_all.25 = bf16[8,32,128]{2,1,0:T(8,128)(2,1)S(1)} all-to-all(bf16[8,32,128]{2,1,0:T(8,128)(2,1)S(1)} %broadcast_in_dim.6), channel_id=1, replica_groups=mesh['z'=8,'w'=2,'x'=4,'c'=2,'y'=4] {'z'}, dimensions={0} | all-to-all | bytes 131072 | tf_op jit(solution)/shard_map/gather_x/all_to_all | solution.py:159
  29.0 0.9 broadcast_in_dim.7
  29.9 0.0 copy-start
  29.9 0.0 copy-start.2
  29.9 4.3 %all-to-all-start.1 = ((bf16[8,8,32,128]{3,2,1,0:T(8,128)(2,1)}), bf16[8,8,32,128]{3,2,1,0:T(8,128)(2,1)S(1)}, u32[]{:S(2)}, u32[]{:S(2)}) async-start(bf16[8,8,32,128]{3,2,1,0:T(8,128)(2,1)} %broadcast_in_dim.7), calls=%async_computation.1 | async-start | bytes 1048576 | tf_op jit(solution)/shard_map/gather_x/all_to_all | solution.py:170
  34.1 0.0 copy-done
  34.1 0.0 copy-start.3
  34.1 4.9 %collective-permute-start.1 = (bf16[2048,128]{1,0:T(8,128)(2,1)S(1)}, bf16[2048,128]{1,0:T(8,128)(2,1)S(1)}, u32[]{:S(2)}, u32[]{:S(2)}) collective-permute-start(bf16[2048,128]{1,0:T(8,128)(2,1)S(1)} %bitcast.3), channel_id=1, source_target_pairs={{0,4},{4,0},{1,5},{5,1},{2,6},{6,2},{3,7},{7,3},{8,12},{12,8},{9,1... | collective-permute-start | bytes 1572872 | tf_op jit(solution)/shard_map/swap_core/ppermute | solution.py:167
  39.7 0.0 copy-done.2
  39.7 0.0 copy-done.3
  39.7 0.6 small.1
  40.3 1.9 %collective-permute-start = (bf16[80,128]{1,0:T(8,128)(2,1)S(1)}, bf16[80,128]{1,0:T(8,128)(2,1)S(1)}, u32[]{:S(2)}, u32[]{:S(2)}) collective-permute-start(bf16[80,128]{1,0:T(8,128)(2,1)S(1)} %small.1), channel_id=1, source_target_pairs={{0,4},{4,0},{1,5},{5,1},{2,6},{6,2},{3,7},{7,3},{8,12},{12,8},{9,1... | collective-permute-start | bytes 61448 | tf_op jit(solution)/shard_map/swap_core/ppermute | solution.py:168
  42.2 1.2 %collective-permute-done.other = bf16[80,128]{1,0:T(8,128)(2,1)S(1)} collective-permute-done((bf16[80,128]{1,0:T(8,128)(2,1)S(1)}, bf16[80,128]{1,0:T(8,128)(2,1)S(1)}, u32[]{:S(2)}, u32[]{:S(2)}) %collective-permute-start) | collective-permute-done | bytes 20512 | tf_op jit(solution)/shard_map/swap_core/ppermute | solution.py:168
  43.3 0.0 collective-permute-done.1.peer
  43.3 0.0 all-to-all-done.1.xg
  43.4 1.3 %agg.1 = (f32[2,32,128]{2,1,0:T(8,128)S(1)}, s32[2,8,128]{2,1,0:T(8,128)S(1)}) custom-call(bf16[80,128]{1,0:T(8,128)(2,1)S(1)} %small.1, bf16[80,128]{1,0:T(8,128)(2,1)S(1)} %collective-permute-done.other, bf16[2048,128]{1,0:T(8,128)(2,1)S(1)} %bitcast.4, bf16[2048,128]{1,0:T(8,128)(2,1)S(1)} %collective-permute-done.1.peer, ...), custom_call_target="tpu_custom_call" | custom-call | tf_op jit(solution)/shard_map/agg/pallas_call | solution.py:30
  44.7 0.0 copy-start.1
  44.7 3.5 %all-gather = f32[4,32,128]{2,1,0:T(8,128)S(1)} all-gather(f32[2,32,128]{2,1,0:T(8,128)S(1)} %get-tuple-element.10), channel_id=2, replica_groups=mesh['z'=8,'w'=2,'x'=4,'c'=2,'y'=4] {'c'}, dimensions={0}, use_global_device_ids=true | all-gather | bytes 98304 | tf_op jit(solution)/shard_map/pair_agg/all_gather | solution.py:179
  48.2 0.0 copy-done.1
  48.3 9.8 %all_to_all.26.got = bf16[4,256,128]{2,1,0:T(8,128)(2,1)S(1)} all-to-all(bf16[4,256,128]{2,1,0:T(8,128)(2,1)S(1)} %ride.1), channel_id=1, replica_groups=mesh['z'=8,'w'=2,'x'=4,'c'=2,'y'=4] {'y'}, dimensions={0} | all-to-all | bytes 524288 | tf_op jit(solution)/shard_map/share_agg/all_to_all | solution.py:187
  58.1 2.4 %back.1 = (bf16[64,128]{1,0:T(8,128)(2,1)}, bf16[8,288,128]{2,1,0:T(8,128)(2,1)S(1)}) custom-call(s32[2,8,128]{2,1,0:T(8,128)S(1)} %get-tuple-element.9.idx, bf16[4,256,128]{2,1,0:T(8,128)(2,1)S(1)} %all_to_all.26.got, bf16[2048,128]{1,0:T(8,128)(2,1)S(1)} %bitcast.5, bf16[2048,128]{1,0:T(8,128)(2,1)S(1)} %collective-permute-done.1.peer), custom_call_target="tpu_custom_call" | custom-call | tf_op jit(solution)/shard_map/back/pallas_call | solution.py:30
  60.5 13.2 %all_to_all.27.got = bf16[8,288,128]{2,1,0:T(8,128)(2,1)S(1)} all-to-all(bf16[8,288,128]{2,1,0:T(8,128)(2,1)S(1)} %get-tuple-element.12), channel_id=1, replica_groups=mesh['z'=8,'w'=2,'x'=4,'c'=2,'y'=4] {'w','x'}, dimensions={0} | all-to-all | bytes 1179648 | tf_op jit(solution)/shard_map/scatter_x/all_to_all | solution.py:196
  73.7 0.1 sum_x.1
  73.8 15.5 %all_to_all.28.got = bf16[8,64,128]{2,1,0:T(8,128)(2,1)S(1)} all-to-all(bf16[8,64,128]{2,1,0:T(8,128)(2,1)S(1)} %sum_x.1), channel_id=1, replica_groups=mesh['z'=8,'w'=2,'x'=4,'c'=2,'y'=4] {'z'}, dimensions={0} | all-to-all | bytes 262144 | tf_op jit(solution)/shard_map/scatter_z/all_to_all | solution.py:199
  89.3 5.2 %all-gather.1 = f32[64,128]{1,0:T(8,128)S(1)} all-gather(f32[32,128]{1,0:T(8,128)S(1)} %half.1), channel_id=3, replica_groups=mesh['z'=8,'w'=2,'x'=4,'c'=2,'y'=4] {'c'}, dimensions={0}, use_global_device_ids=true | all-gather | bytes 49152 | tf_op jit(solution)/shard_map/join_w/all_gather | solution.py:202
  94.5 0.6 last.1
  (2 shorter events, 0.0 us)
Async XLA Ops:
  29.9 4.3 %copy-start = (bf16[1,16,128,128]{3,2,1,0:T(8,128)(2,1)S(1)}, bf16[1,16,128,128]{3,2,1,0:T(8,128)(2,1)}, u32[]{:S(2)}) copy-start(bf16[1,16,128,128]{3,2,1,0:T(8,128)(2,1)} %param.10) | copy-start | bytes 1572868
  29.9 9.8 %copy-start.2 = (bf16[64,128]{1,0:T(8,128)(2,1)S(1)}, bf16[64,128]{1,0:T(8,128)(2,1)}, u32[]{:S(2)}) copy-start(bf16[64,128]{1,0:T(8,128)(2,1)} %d_out.1) | copy-start | bytes 49156
  29.9 13.5 %all-to-all-start.1 = ((bf16[8,8,32,128]{3,2,1,0:T(8,128)(2,1)}), bf16[8,8,32,128]{3,2,1,0:T(8,128)(2,1)S(1)}, u32[]{:S(2)}, u32[]{:S(2)}) async-start(bf16[8,8,32,128]{3,2,1,0:T(8,128)(2,1)} %broadcast_in_dim.7), calls=%async_computation.1 | async-start | bytes 1048576 | tf_op jit(solution)/shard_map/gather_x/all_to_all | solution.py:170
  34.1 5.6 %copy-start.3 = (s32[1,16]{1,0:T(1,128)S(1)}, s32[1,16]{1,0:T(1,128)}, u32[]{:S(2)}) copy-start(s32[1,16]{1,0:T(1,128)} %cols.1) | copy-start | bytes 196
  34.1 9.2 %collective-permute-start.1 = (bf16[2048,128]{1,0:T(8,128)(2,1)S(1)}, bf16[2048,128]{1,0:T(8,128)(2,1)S(1)}, u32[]{:S(2)}, u32[]{:S(2)}) collective-permute-start(bf16[2048,128]{1,0:T(8,128)(2,1)S(1)} %bitcast.3), channel_id=1, source_target_pairs={{0,4},{4,0},{1,5},{5,1},{2,6},{6,2},{3,7},{7,3},{8,12},{12,8},{9,1... | collective-permute-start | bytes 1572872 | tf_op jit(solution)/shard_map/swap_core/ppermute | solution.py:167
  40.3 3.1 %collective-permute-start = (bf16[80,128]{1,0:T(8,128)(2,1)S(1)}, bf16[80,128]{1,0:T(8,128)(2,1)S(1)}, u32[]{:S(2)}, u32[]{:S(2)}) collective-permute-start(bf16[80,128]{1,0:T(8,128)(2,1)S(1)} %small.1), channel_id=1, source_target_pairs={{0,4},{4,0},{1,5},{5,1},{2,6},{6,2},{3,7},{7,3},{8,12},{12,8},{9,1... | collective-permute-start | bytes 61448 | tf_op jit(solution)/shard_map/swap_core/ppermute | solution.py:168
  44.7 3.5 %copy-start.1 = (bf16[32,256]{1,0:T(8,128)(2,1)S(1)}, bf16[32,256]{1,0:T(8,128)(2,1)}, u32[]{:S(2)}) copy-start(bf16[32,256]{1,0:T(8,128)(2,1)} %weight.1) | copy-start | bytes 49156

commit v5 on v4

--- a/solution.py
+++ b/solution.py
@@ -10,13 +10,14 @@
 NZ, NW, NX, NC, NY = 8, 2, 4, 2, 4
 NP = NW * NX
 K, B, FL, HL = 16, 128, 32, 64
-SMALL = HL + 16
+D_OUT, META, MINE = K * B, K * B + HL, K * B + HL + 16
 RIDE = NC * FL + NC * HL + 2 * FL
-D_AT, W_AT = NC * FL, NC * FL + NC * HL
+C_AT, W_AT = NC * FL, NC * FL + NC * HL
 C0, C1 = 0.7978845608, 0.044715
 VM = pltpu.CompilerParams(vmem_limit_bytes=32 * 1024 * 1024)
 VMEM = pl.BlockSpec(memory_space=pltpu.VMEM)
 SMEM = pl.BlockSpec(memory_space=pltpu.SMEM)
+HBM = pl.BlockSpec(memory_space=pl.ANY)
 
 
 def dot(a, b, ca, cb):
@@ -38,19 +39,20 @@
     )(*args)
 
 
-def small_kernel(cols, count, d_out, out):
-    lane = lax.broadcasted_iota(jnp.int32, (16, B), 1)
-    meta = jnp.where(lane == K, count[0], 0)
-    for s in range(K):
-        meta = jnp.where(lane == s, cols[0, s], meta)
-    out[0:HL, :] = d_out[...]
-    out[HL:, :] = meta.astype(F32).astype(BF)
-
-
-def agg_kernel(small, other, mine, peer, xg, out, idx, ints, sem):
+def pack_kernel(meta, d_out, vals, mine, sems):
+    parts = ((vals, mine.at[0:D_OUT]), (d_out, mine.at[D_OUT:META]))
+    copies = [pltpu.make_async_copy(*part, sems.at[i]) for i, part in enumerate(parts)]
+    for copy in copies:
+        copy.start()
+    mine[META:, :] = meta[...].astype(F32).astype(BF)
+    for copy in copies:
+        copy.wait()
+
+
+def agg_kernel(mine, peer, xg, out, idx, ints, sem):
     core = lax.axis_index("c")
-    for r, got in enumerate((small, other)):
-        idx[r] = got[HL:, :].astype(F32)[0:8].astype(jnp.int32)
+    for r, got in enumerate((mine, peer)):
+        idx[r] = got[META:, :].astype(F32)[0:8].astype(jnp.int32)
     copy = pltpu.make_async_copy(idx, ints, sem)
     copy.start()
     copy.wait()
@@ -65,17 +67,18 @@
         out[r] = acc
 
 
-def ride_kernel(parts, small, other, weight, out):
+def ride_kernel(parts, mine, peer, weight, out):
     core = lax.axis_index("c")
     for y in range(NY):
         out[y, W_AT : W_AT + FL, :] = weight[:, :B]
         out[y, W_AT + FL :, :] = weight[:, B:]
     for c in range(NC):
         agg = (parts[c, 0] + parts[1 - c, 1]).astype(BF)
-        cot = jnp.where(core == c, small[0:HL, :].astype(F32), other[0:HL, :].astype(F32))
+        cot = [got[D_OUT:META, :].astype(F32) for got in (mine, peer)]
+        cot = jnp.where(core == c, *cot)
         for y in range(NY):
             out[y, c * FL : (c + 1) * FL, :] = agg
-            out[y, D_AT + c * HL : D_AT + (c + 1) * HL, :] = cot.astype(BF)
+            out[y, C_AT + c * HL : C_AT + (c + 1) * HL, :] = cot.astype(BF)
 
 
 def back_kernel(idx, got, mine, peer, out_t, out, term, hidden):
@@ -107,7 +110,7 @@
         cot = jnp.concatenate(
             [
                 jnp.concatenate(
-                    [got[2 * h + q, D_AT + c * HL : D_AT + (c + 1) * HL, :] for q in range(2)],
+                    [got[2 * h + q, C_AT + c * HL : C_AT + (c + 1) * HL, :] for q in range(2)],
                     axis=0,
                 )
                 for c in range(NC)
@@ -154,25 +157,29 @@
 
 
 def local(x_t, weight, block_cols, block_count, block_vals, d_out_t):
-    mine = block_vals.reshape(K * B, B)
     with jax.named_scope("gather_x"):
         a = lax.all_to_all(jnp.broadcast_to(x_t, (NZ, FL, B)), "z", 0, 0, tiled=True)
-    small = call(
-        small_kernel,
-        ((SMALL, B), BF),
-        "small",
-        [(SMEM, block_cols), (SMEM, block_count), (VMEM, d_out_t)],
+    meta = jnp.concatenate([block_cols, block_count[:, None]], axis=1)
+    mine = call(
+        pack_kernel,
+        ((MINE, B), BF),
+        "pack",
+        [
+            (VMEM, jnp.pad(meta, ((0, 15), (0, B - K - 1)))),
+            (HBM, d_out_t),
+            (HBM, block_vals.reshape(K * B, B)),
+        ],
+        [pltpu.SemaphoreType.DMA((2,))],
     )
     with jax.named_scope("swap_core"):
         peer = lax.ppermute(mine, "c", [(0, 1), (1, 0)])
-        other = lax.ppermute(small, "c", [(0, 1), (1, 0)])
     with jax.named_scope("gather_x"):
         a = lax.all_to_all(jnp.broadcast_to(a, (NP, NZ, FL, B)), ("w", "x"), 0, 0, tiled=True)
     parts, idx = call(
         agg_kernel,
         [((NC, FL, B), F32), ((NC, 8, B), jnp.int32)],
         "agg",
-        [(VMEM, small), (VMEM, other), (VMEM, mine), (VMEM, peer), (VMEM, a)],
+        [(VMEM, mine), (VMEM, peer), (VMEM, a)],
         [pltpu.SMEM((NC, 8, B), jnp.int32), pltpu.SemaphoreType.DMA],
     )
     with jax.named_scope("pair_agg"):
@@ -181,7 +188,7 @@
         ride_kernel,
         ((NY, RIDE, B), BF),
         "ride",
-        [(VMEM, parts), (VMEM, small), (VMEM, other), (VMEM, weight)],
+        [(VMEM, parts), (VMEM, mine), (VMEM, peer), (VMEM, weight)],
     )
     with jax.named_scope("share_agg"):
         ride = lax.all_to_all(ride, "y", 0, 0, tiled=True)

time: 95.6 us -> 94.3 us (0.986)
  starting transfers between devices: 11.1 us -> 9.15 us
    all_gather x1, blocking collectives: 3.53 us -> 5.47 us  [local(): parts = lax.all_gather(parts, 'c', axis=0, tiled=False)]
    ppermute x1 -> x0, starting transfers between devices: 1.92 us -> none  [local(): other = lax.ppermute(small, 'c', [(0, 1), (1, 0)])]
    all_to_all x1, blocking collectives: 13.2 us -> 11.3 us  [local(): term = lax.all_to_all(term, ('w', 'x'), 0, 0, tiled=True)]
    ppermute x1, waiting for transfers between devices: 0.01 us -> 1.54 us  [local(): peer = lax.ppermute(mine, 'c', [(0, 1), (1, 0)])]
    ppermute x1 -> x0, waiting for transfers between devices: 1.16 us -> none  [local(): other = lax.ppermute(small, 'c', [(0, 1), (1, 0)])]
  transfers between devices with their start and end apart: 3 -> 2, of which waited for: 1 -> 1; matrix products, arithmetic and copies ran while one was open for 0% -> 0% of each run, Pallas kernels for 1% -> 0%
where the time goes in v5:
time: 94.3 us; the launch traced here: 93.8 us
  blocking collectives  75.5 us (80%)
  starting transfers between devices  9.15 us (10%)
  Pallas kernels  4.51 us (5%)
  local copies, waits for them, and re-layouts  1.62 us (2%)
  waiting for transfers between devices  1.55 us (2%)
  between operations  1.35 us (1%)
    all_to_all x1, blocking collectives, local(): lax.all_to_all(jnp.broadcast_to(x_t, (NZ, FL, B)), 'z', 0, 0, tiled=True)  27.6 us
    all_to_all x1, blocking collectives, local(): term = lax.all_to_all(term, 'z', 0, 0, tiled=True)  15.4 us
    all_to_all x1, blocking collectives, local(): term = lax.all_to_all(term, ('w', 'x'), 0, 0, tiled=True)  11.3 us
    all_to_all x1, blocking collectives, local(): ride = lax.all_to_all(ride, 'y', 0, 0, tiled=True)  9.82 us
    all_gather x1, blocking collectives, local(): halves = lax.all_gather(half, 'c', axis=0, tiled=False)  5.81 us
    all_gather x1, blocking collectives, local(): parts = lax.all_gather(parts, 'c', axis=0, tiled=False)  5.47 us
    ppermute x1, starting transfers between devices, local(): peer = lax.ppermute(mine, 'c', [(0, 1), (1, 0)])  4.89 us
    pallas_call x7, Pallas kernels, call(): pl.pallas_call(kernel, out_shape=shapes[0] if one else tuple(shapes), in_...  4.51 us
  transfers between devices with their start and end apart: 2, of which 1 were waited for; matrix products, arithmetic and copies ran while one was open for 0% of the time, Pallas kernels for 0%

profile of v5, /device:TPU:1, one launch (start us, length us, event | category | flops | bytes accessed | tf_op | source)
XLA Modules:
  0.0 93.8 jit_solution(3038043269796963519)
XLA Ops:
  0.6 0.7 broadcast_in_dim.10
  1.3 27.6 %all_to_all.25 = bf16[8,32,128]{2,1,0:T(8,128)(2,1)S(1)} all-to-all(bf16[8,32,128]{2,1,0:T(8,128)(2,1)S(1)} %broadcast_in_dim.10), channel_id=1, replica_groups=mesh['z'=8,'w'=2,'x'=4,'c'=2,'y'=4] {'z'}, dimensions={0} | all-to-all | bytes 131072 | tf_op jit(solution)/shard_map/gather_x/all_to_all | solution.py:161
  29.0 0.9 broadcast_in_dim.11
  29.9 0.0 copy-start.3
  29.9 0.0 copy-start
  29.9 4.3 %all-to-all-start.1 = ((bf16[8,8,32,128]{3,2,1,0:T(8,128)(2,1)}), bf16[8,8,32,128]{3,2,1,0:T(8,128)(2,1)S(1)}, u32[]{:S(2)}, u32[]{:S(2)}) async-start(bf16[8,8,32,128]{3,2,1,0:T(8,128)(2,1)} %broadcast_in_dim.11), calls=%async_computation.1 | async-start | bytes 1048576 | tf_op jit(solution)/shard_map/gather_x/all_to_all | solution.py:177
  34.1 0.0 copy-start.1
  34.8 0.0 copy-done.3
  34.8 0.1 pad_add_fusion
  34.9 0.0 copy-done
  34.9 0.0 copy-done.1
  34.9 0.1 pack.1.mine
  35.0 4.9 %collective-permute-start = (bf16[2128,128]{1,0:T(8,128)(2,1)S(1)}, bf16[2128,128]{1,0:T(8,128)(2,1)S(1)}, u32[]{:S(2)}, u32[]{:S(2)}) collective-permute-start(bf16[2128,128]{1,0:T(8,128)(2,1)S(1)} %pack.1.mine), channel_id=1, source_target_pairs={{0,4},{4,0},{1,5},{5,1},{2,6},{6,2},{3,7},{7,3},{8,12},{12,8},{9,1... | collective-permute-start | bytes 1634312 | tf_op jit(solution)/shard_map/swap_core/ppermute | solution.py:175
  39.9 1.5 %collective-permute-done.peer = bf16[2128,128]{1,0:T(8,128)(2,1)S(1)} collective-permute-done((bf16[2128,128]{1,0:T(8,128)(2,1)S(1)}, bf16[2128,128]{1,0:T(8,128)(2,1)S(1)}, u32[]{:S(2)}, u32[]{:S(2)}) %collective-permute-start) | collective-permute-done | bytes 544800 | tf_op jit(solution)/shard_map/swap_core/ppermute | solution.py:175
  41.4 0.0 all-to-all-done.1.xg
  41.4 1.3 %agg.1 = (f32[2,32,128]{2,1,0:T(8,128)S(1)}, s32[2,8,128]{2,1,0:T(8,128)S(1)}) custom-call(bf16[2128,128]{1,0:T(8,128)(2,1)S(1)} %pack.1.mine, bf16[2128,128]{1,0:T(8,128)(2,1)S(1)} %collective-permute-done.peer, bf16[8,8,32,128]{3,2,1,0:T(8,128)(2,1)S(1)} %all-to-all-done.1.xg), custom_call_target="tpu_custom_call" | custom-call | tf_op jit(solution)/shard_map/agg/pallas_call | solution.py:31
  42.8 0.0 copy-start.2
  42.8 5.5 %all-gather = f32[4,32,128]{2,1,0:T(8,128)S(1)} all-gather(f32[2,32,128]{2,1,0:T(8,128)S(1)} %get-tuple-element.10), channel_id=2, replica_groups=mesh['z'=8,'w'=2,'x'=4,'c'=2,'y'=4] {'c'}, dimensions={0}, use_global_device_ids=true | all-gather | bytes 98304 | tf_op jit(solution)/shard_map/pair_agg/all_gather | solution.py:186
  48.2 0.0 copy-done.2
  48.3 9.8 %all_to_all.26.got = bf16[4,256,128]{2,1,0:T(8,128)(2,1)S(1)} all-to-all(bf16[4,256,128]{2,1,0:T(8,128)(2,1)S(1)} %ride.1), channel_id=1, replica_groups=mesh['z'=8,'w'=2,'x'=4,'c'=2,'y'=4] {'y'}, dimensions={0} | all-to-all | bytes 524288 | tf_op jit(solution)/shard_map/share_agg/all_to_all | solution.py:194
  58.1 2.4 %back.1 = (bf16[64,128]{1,0:T(8,128)(2,1)}, bf16[8,288,128]{2,1,0:T(8,128)(2,1)S(1)}) custom-call(s32[2,8,128]{2,1,0:T(8,128)S(1)} %get-tuple-element.9.idx, bf16[4,256,128]{2,1,0:T(8,128)(2,1)S(1)} %all_to_all.26.got, bf16[2128,128]{1,0:T(8,128)(2,1)S(1)} %pack.1.mine, bf16[2128,128]{1,0:T(8,128)(2,1)S(1)} %collective-permute-done.peer), custom_call_target="tpu_custom_call" | custom-call | tf_op jit(solution)/shard_map/back/pallas_call | solution.py:31
  60.5 11.3 %all_to_all.27.got = bf16[8,288,128]{2,1,0:T(8,128)(2,1)S(1)} all-to-all(bf16[8,288,128]{2,1,0:T(8,128)(2,1)S(1)} %get-tuple-element.12), channel_id=1, replica_groups=mesh['z'=8,'w'=2,'x'=4,'c'=2,'y'=4] {'w','x'}, dimensions={0} | all-to-all | bytes 1179648 | tf_op jit(solution)/shard_map/scatter_x/all_to_all | solution.py:203
  71.8 0.1 sum_x.1
  71.9 15.4 %all_to_all.28.got = bf16[8,64,128]{2,1,0:T(8,128)(2,1)S(1)} all-to-all(bf16[8,64,128]{2,1,0:T(8,128)(2,1)S(1)} %sum_x.1), channel_id=1, replica_groups=mesh['z'=8,'w'=2,'x'=4,'c'=2,'y'=4] {'z'}, dimensions={0} | all-to-all | bytes 262144 | tf_op jit(solution)/shard_map/scatter_z/all_to_all | solution.py:206
  87.3 5.8 %all-gather.1 = f32[64,128]{1,0:T(8,128)S(1)} all-gather(f32[32,128]{1,0:T(8,128)S(1)} %half.1), channel_id=3, replica_groups=mesh['z'=8,'w'=2,'x'=4,'c'=2,'y'=4] {'c'}, dimensions={0}, use_global_device_ids=true | all-gather | bytes 49152 | tf_op jit(solution)/shard_map/join_w/all_gather | solution.py:209
  93.1 0.6 last.1
  (3 shorter events, 0.0 us)
Async XLA Ops:
  29.9 4.9 %copy-start.3 = (s32[1,16]{1,0:T(1,128)S(1)}, s32[1,16]{1,0:T(1,128)}, u32[]{:S(2)}) copy-start(s32[1,16]{1,0:T(1,128)} %param.8) | copy-start | bytes 196
  29.9 5.0 %copy-start = (bf16[1,16,128,128]{3,2,1,0:T(8,128)(2,1)S(1)}, bf16[1,16,128,128]{3,2,1,0:T(8,128)(2,1)}, u32[]{:S(2)}) copy-start(bf16[1,16,128,128]{3,2,1,0:T(8,128)(2,1)} %param.10) | copy-start | bytes 1572868
  29.9 11.6 %all-to-all-start.1 = ((bf16[8,8,32,128]{3,2,1,0:T(8,128)(2,1)}), bf16[8,8,32,128]{3,2,1,0:T(8,128)(2,1)S(1)}, u32[]{:S(2)}, u32[]{:S(2)}) async-start(bf16[8,8,32,128]{3,2,1,0:T(8,128)(2,1)} %broadcast_in_dim.11), calls=%async_computation.1 | async-start | bytes 1048576 | tf_op jit(solution)/shard_map/gather_x/all_to_all | solution.py:177
  34.1 0.8 copy-start.1
  35.0 6.4 %collective-permute-start = (bf16[2128,128]{1,0:T(8,128)(2,1)S(1)}, bf16[2128,128]{1,0:T(8,128)(2,1)S(1)}, u32[]{:S(2)}, u32[]{:S(2)}) collective-permute-start(bf16[2128,128]{1,0:T(8,128)(2,1)S(1)} %pack.1.mine), channel_id=1, source_target_pairs={{0,4},{4,0},{1,5},{5,1},{2,6},{6,2},{3,7},{7,3},{8,12},{12,8},{9,1... | collective-permute-start | bytes 1634312 | tf_op jit(solution)/shard_map/swap_core/ppermute | solution.py:175
  42.8 5.5 %copy-start.2 = (bf16[32,256]{1,0:T(8,128)(2,1)S(1)}, bf16[32,256]{1,0:T(8,128)(2,1)}, u32[]{:S(2)}) copy-start(bf16[32,256]{1,0:T(8,128)(2,1)} %weight.1) | copy-start | bytes 49156

commit v6 on v5

--- a/solution.py
+++ b/solution.py
@@ -49,18 +49,13 @@
         copy.wait()
 
 
-def agg_kernel(mine, peer, xg, out, idx, ints, sem):
+def agg_kernel(my_idx, peer_idx, mine, peer, xg, out):
     core = lax.axis_index("c")
-    for r, got in enumerate((mine, peer)):
-        idx[r] = got[META:, :].astype(F32)[0:8].astype(jnp.int32)
-    copy = pltpu.make_async_copy(idx, ints, sem)
-    copy.start()
-    copy.wait()
-    for r, blocks in enumerate((mine, peer)):
+    for r, (idx, blocks) in enumerate(((my_idx, mine), (peer_idx, peer))):
         acc = jnp.zeros((FL, B), F32)
         for s in range(K):
-            owner = ints[r, 0, s]
-            use = jnp.logical_and(owner % NC == core, s < ints[r, 0, K])
+            owner = idx[s]
+            use = jnp.logical_and(owner % NC == core, s < idx[K])
             got = xg[(owner // NC) % NP, owner // (NC * NP)]
             got = jnp.where(use, got, jnp.zeros_like(got))
             acc = acc + dot(got, blocks[s * B : (s + 1) * B, :], 1, 1)
@@ -81,7 +76,13 @@
             out[y, C_AT + c * HL : C_AT + (c + 1) * HL, :] = cot.astype(BF)
 
 
-def back_kernel(idx, got, mine, peer, out_t, out, term, hidden):
+def back_kernel(idx_a, idx_b, got, mine, peer, out_t, out, term, hidden, my_idx, peer_idx, sems):
+    copies = [
+        pltpu.make_async_copy(src, dst, sems.at[i])
+        for i, (src, dst) in enumerate(((idx_a, my_idx), (idx_b, peer_idx)))
+    ]
+    for copy in copies:
+        copy.start()
     core, y_at = lax.axis_index("c"), lax.axis_index("y")
     term[...] = jnp.zeros_like(term)
     agg = jnp.concatenate(
@@ -122,13 +123,15 @@
         back = back + dot(got[y_at, rows, :], grad, 1, 0)
     gw = dot(own, hidden[core], 1, 1).astype(BF)
     back = back.astype(BF)
-    for r, blocks in enumerate((mine, peer)):
+    for copy in copies:
+        copy.wait()
+    for r, (idx, blocks) in enumerate(((my_idx, mine), (peer_idx, peer))):
         mix = back[:, :B], back[:, B:]
         first = core == 0 if r == 0 else core == 1
         grad = jnp.where(first, mix[0], mix[1])
         for s in range(K):
-            owner = idx[r, 0, s]
-            use = jnp.logical_and(owner % NC == core, s < idx[r, 0, K])
+            owner = idx[s]
+            use = jnp.logical_and(owner % NC == core, s < idx[K])
             at = ((owner // NC) % NP) * NZ + owner // (NC * NP)
             at = jnp.where(use, at, NP * NZ)
             term[at] = term[at] + dot(grad, blocks[s * B : (s + 1) * B, :], 1, 0)
@@ -175,12 +178,13 @@
         peer = lax.ppermute(mine, "c", [(0, 1), (1, 0)])
     with jax.named_scope("gather_x"):
         a = lax.all_to_all(jnp.broadcast_to(a, (NP, NZ, FL, B)), ("w", "x"), 0, 0, tiled=True)
-    parts, idx = call(
+    my_idx = meta[0]
+    peer_idx = peer[META, : K + 1].astype(jnp.int32)
+    parts = call(
         agg_kernel,
-        [((NC, FL, B), F32), ((NC, 8, B), jnp.int32)],
+        ((NC, FL, B), F32),
         "agg",
-        [(VMEM, mine), (VMEM, peer), (VMEM, a)],
-        [pltpu.SMEM((NC, 8, B), jnp.int32), pltpu.SemaphoreType.DMA],
+        [(SMEM, my_idx), (SMEM, peer_idx), (VMEM, mine), (VMEM, peer), (VMEM, a)],
     )
     with jax.named_scope("pair_agg"):
         parts = lax.all_gather(parts, "c", axis=0, tiled=False)
@@ -196,8 +200,10 @@
         back_kernel,
         [((HL, B), BF), ((NP, NZ * FL + FL, B), BF)],
         "back",
-        [(SMEM, idx), (VMEM, ride), (VMEM, mine), (VMEM, peer)],
-        [pltpu.VMEM((NP * NZ + 1, FL, B), F32), pltpu.VMEM((2, B, NC * B), BF)],
+        [(HBM, my_idx), (HBM, peer_idx), (VMEM, ride), (VMEM, mine), (VMEM, peer)],
+        [pltpu.VMEM((NP * NZ + 1, FL, B), F32), pltpu.VMEM((2, B, NC * B), BF)]
+        + [pltpu.SMEM((K + 1,), jnp.int32)] * 2
+        + [pltpu.SemaphoreType.DMA((2,))],
     )
     with jax.named_scope("scatter_x"):
         term = lax.all_to_all(term, ("w", "x"), 0, 0, tiled=True)

time: 94.3 us -> 93.8 us (level)
  no operation moved by 1% of the time
where the time goes in v6:
time: 93.8 us; the launch traced here: 93.2 us
  blocking collectives  75.7 us (81%)
  starting transfers between devices  9.15 us (10%)
  Pallas kernels  3.83 us (4%)
  local copies, waits for them, and re-layouts  1.62 us (2%)
  waiting for transfers between devices  1.47 us (2%)
  between operations  1.34 us (1%)
    all_to_all x1, blocking collectives, local(): lax.all_to_all(jnp.broadcast_to(x_t, (NZ, FL, B)), 'z', 0, 0, tiled=True)  27.6 us
    all_to_all x1, blocking collectives, local(): term = lax.all_to_all(term, 'z', 0, 0, tiled=True)  15.4 us
    all_to_all x1, blocking collectives, local(): term = lax.all_to_all(term, ('w', 'x'), 0, 0, tiled=True)  11.4 us
    all_to_all x1, blocking collectives, local(): ride = lax.all_to_all(ride, 'y', 0, 0, tiled=True)  9.82 us
    all_gather x1, blocking collectives, local(): halves = lax.all_gather(half, 'c', axis=0, tiled=False)  5.82 us
    all_gather x1, blocking collectives, local(): parts = lax.all_gather(parts, 'c', axis=0, tiled=False)  5.6 us
    ppermute x1, starting transfers between devices, local(): peer = lax.ppermute(mine, 'c', [(0, 1), (1, 0)])  4.89 us
    all_to_all x1, starting transfers between devices, local(): lax.all_to_all(jnp.broadcast_to(a, (NP, NZ, FL, B)), ('w', 'x'), 0, 0, ti...  4.26 us
  transfers between devices with their start and end apart: 2, of which 1 were waited for; matrix products, arithmetic and copies ran while one was open for 0% of the time, Pallas kernels for 0%

profile of v6, /device:TPU:1, one launch (start us, length us, event | category | flops | bytes accessed | tf_op | source)
XLA Modules:
  0.0 93.2 jit_solution(8701833963085294854)
XLA Ops:
  0.6 0.7 broadcast_in_dim.10
  1.3 27.6 %all_to_all.25 = bf16[8,32,128]{2,1,0:T(8,128)(2,1)S(1)} all-to-all(bf16[8,32,128]{2,1,0:T(8,128)(2,1)S(1)} %broadcast_in_dim.10), channel_id=1, replica_groups=mesh['z'=8,'w'=2,'x'=4,'c'=2,'y'=4] {'z'}, dimensions={0} | all-to-all | bytes 131072 | tf_op jit(solution)/shard_map/gather_x/all_to_all | solution.py:164
  29.0 0.9 broadcast_in_dim.11
  29.9 0.0 copy-start.3
  29.9 0.0 copy-start
  29.9 4.3 %all-to-all-start.1 = ((bf16[8,8,32,128]{3,2,1,0:T(8,128)(2,1)}), bf16[8,8,32,128]{3,2,1,0:T(8,128)(2,1)S(1)}, u32[]{:S(2)}, u32[]{:S(2)}) async-start(bf16[8,8,32,128]{3,2,1,0:T(8,128)(2,1)} %broadcast_in_dim.11), calls=%async_computation.1 | async-start | bytes 1048576 | tf_op jit(solution)/shard_map/gather_x/all_to_all | solution.py:180
  34.1 0.0 copy-start.1
  34.8 0.0 copy-done.3
  34.8 0.1 pad_add_fusion
  34.9 0.0 copy-done
  34.9 0.0 copy-done.1
  34.9 0.1 pack.1.mine
  35.0 4.9 %collective-permute-start = (bf16[2128,128]{1,0:T(8,128)(2,1)S(1)}, bf16[2128,128]{1,0:T(8,128)(2,1)S(1)}, u32[]{:S(2)}, u32[]{:S(2)}) collective-permute-start(bf16[2128,128]{1,0:T(8,128)(2,1)S(1)} %pack.1.mine), channel_id=1, source_target_pairs={{0,4},{4,0},{1,5},{5,1},{2,6},{6,2},{3,7},{7,3},{8,12},{12,8},{9,1... | collective-permute-start | bytes 1634312 | tf_op jit(solution)/shard_map/swap_core/ppermute | solution.py:178
  39.9 0.1 fusion.1.my_idx.idx_a
  40.0 1.5 %collective-permute-done.peer = bf16[2128,128]{1,0:T(8,128)(2,1)S(1)} collective-permute-done((bf16[2128,128]{1,0:T(8,128)(2,1)S(1)}, bf16[2128,128]{1,0:T(8,128)(2,1)S(1)}, u32[]{:S(2)}, u32[]{:S(2)}) %collective-permute-start) | collective-permute-done | bytes 544800 | tf_op jit(solution)/shard_map/swap_core/ppermute | solution.py:178
  41.4 0.0 all-to-all-done.1.xg
  41.4 1.2 %agg.1 = f32[2,32,128]{2,1,0:T(8,128)S(1)} custom-call(s32[17]{0:T(128)S(1)} %fusion.1.my_idx.idx_a, s32[17]{0:T(128)S(1)} %fusion.peer_idx.idx_b, bf16[2128,128]{1,0:T(8,128)(2,1)S(1)} %pack.1.mine, bf16[2128,128]{1,0:T(8,128)(2,1)S(1)} %collective-permute-done.peer, bf16[8,8,32,128]{3,2,1,0:T(8,128)(2,1)S(1)} %all-to-all-done.1.xg), custom_call_target="tpu_custom_call" | custom-call | tf_op jit(solution)/shard_map/agg/pallas_call | solution.py:31
  42.6 0.0 copy-start.2
  42.6 5.6 %all-gather = f32[4,32,128]{2,1,0:T(8,128)S(1)} all-gather(f32[2,32,128]{2,1,0:T(8,128)S(1)} %agg.1), channel_id=2, replica_groups=mesh['z'=8,'w'=2,'x'=4,'c'=2,'y'=4] {'c'}, dimensions={0}, use_global_device_ids=true | all-gather | bytes 98304 | tf_op jit(solution)/shard_map/pair_agg/all_gather | solution.py:190
  48.2 0.0 copy-done.2
  48.3 9.8 %all_to_all.26.got = bf16[4,256,128]{2,1,0:T(8,128)(2,1)S(1)} all-to-all(bf16[4,256,128]{2,1,0:T(8,128)(2,1)S(1)} %ride.1), channel_id=1, replica_groups=mesh['z'=8,'w'=2,'x'=4,'c'=2,'y'=4] {'y'}, dimensions={0} | all-to-all | bytes 524288 | tf_op jit(solution)/shard_map/share_agg/all_to_all | solution.py:198
  58.1 1.8 %back.1 = (bf16[64,128]{1,0:T(8,128)(2,1)}, bf16[8,288,128]{2,1,0:T(8,128)(2,1)S(1)}) custom-call(s32[17]{0:T(128)S(1)} %fusion.1.my_idx.idx_a, s32[17]{0:T(128)S(1)} %fusion.peer_idx.idx_b, bf16[4,256,128]{2,1,0:T(8,128)(2,1)S(1)} %all_to_all.26.got, bf16[2128,128]{1,0:T(8,128)(2,1)S(1)} %pack.1.mine, bf16[2128,128]{1,0:T(8,128)(2,1)S(1)} %collective-permute-done.peer), custom_call_target="tpu_custom_call" | custom-call | tf_op jit(solution)/shard_map/back/pallas_call | solution.py:31
  59.9 11.4 %all_to_all.27.got = bf16[8,288,128]{2,1,0:T(8,128)(2,1)S(1)} all-to-all(bf16[8,288,128]{2,1,0:T(8,128)(2,1)S(1)} %get-tuple-element.8), channel_id=1, replica_groups=mesh['z'=8,'w'=2,'x'=4,'c'=2,'y'=4] {'w','x'}, dimensions={0} | all-to-all | bytes 1179648 | tf_op jit(solution)/shard_map/scatter_x/all_to_all | solution.py:209
  71.3 0.1 sum_x.1
  71.3 15.4 %all_to_all.28.got = bf16[8,64,128]{2,1,0:T(8,128)(2,1)S(1)} all-to-all(bf16[8,64,128]{2,1,0:T(8,128)(2,1)S(1)} %sum_x.1), channel_id=1, replica_groups=mesh['z'=8,'w'=2,'x'=4,'c'=2,'y'=4] {'z'}, dimensions={0} | all-to-all | bytes 262144 | tf_op jit(solution)/shard_map/scatter_z/all_to_all | solution.py:212
  86.8 5.8 %all-gather.1 = f32[64,128]{1,0:T(8,128)S(1)} all-gather(f32[32,128]{1,0:T(8,128)S(1)} %half.1), channel_id=3, replica_groups=mesh['z'=8,'w'=2,'x'=4,'c'=2,'y'=4] {'c'}, dimensions={0}, use_global_device_ids=true | all-gather | bytes 49152 | tf_op jit(solution)/shard_map/join_w/all_gather | solution.py:215
  92.6 0.6 last.1
  (4 shorter events, 0.1 us)
Async XLA Ops:
  29.9 4.9 %copy-start.3 = (s32[1,16]{1,0:T(1,128)S(1)}, s32[1,16]{1,0:T(1,128)}, u32[]{:S(2)}) copy-start(s32[1,16]{1,0:T(1,128)} %param.8) | copy-start | bytes 196
  29.9 5.0 %copy-start = (bf16[1,16,128,128]{3,2,1,0:T(8,128)(2,1)S(1)}, bf16[1,16,128,128]{3,2,1,0:T(8,128)(2,1)}, u32[]{:S(2)}) copy-start(bf16[1,16,128,128]{3,2,1,0:T(8,128)(2,1)} %param.10) | copy-start | bytes 1572868
  29.9 11.6 %all-to-all-start.1 = ((bf16[8,8,32,128]{3,2,1,0:T(8,128)(2,1)}), bf16[8,8,32,128]{3,2,1,0:T(8,128)(2,1)S(1)}, u32[]{:S(2)}, u32[]{:S(2)}) async-start(bf16[8,8,32,128]{3,2,1,0:T(8,128)(2,1)} %broadcast_in_dim.11), calls=%async_computation.1 | async-start | bytes 1048576 | tf_op jit(solution)/shard_map/gather_x/all_to_all | solution.py:180
  34.1 0.8 copy-start.1
  35.0 6.4 %collective-permute-start = (bf16[2128,128]{1,0:T(8,128)(2,1)S(1)}, bf16[2128,128]{1,0:T(8,128)(2,1)S(1)}, u32[]{:S(2)}, u32[]{:S(2)}) collective-permute-start(bf16[2128,128]{1,0:T(8,128)(2,1)S(1)} %pack.1.mine), channel_id=1, source_target_pairs={{0,4},{4,0},{1,5},{5,1},{2,6},{6,2},{3,7},{7,3},{8,12},{12,8},{9,1... | collective-permute-start | bytes 1634312 | tf_op jit(solution)/shard_map/swap_core/ppermute | solution.py:178
  42.6 5.6 %copy-start.2 = (bf16[32,256]{1,0:T(8,128)(2,1)S(1)}, bf16[32,256]{1,0:T(8,128)(2,1)}, u32[]{:S(2)}) copy-start(bf16[32,256]{1,0:T(8,128)(2,1)} %weight.1) | copy-start | bytes 49156

commit v7 on v6

--- a/solution.py
+++ b/solution.py
@@ -24,7 +24,7 @@
     return lax.dot_general(a, b, (((ca,), (cb,)), ((), ())), preferred_element_type=F32)
 
 
-def call(kernel, outs, name, ins, scratch=()):
+def call(kernel, outs, name, ins, scratch=(), spaces=None):
     specs, args = zip(*ins)
     one = not isinstance(outs, list)
     shapes = [jax.ShapeDtypeStruct(*o) for o in ((outs,) if one else outs)]
@@ -32,7 +32,7 @@
         kernel,
         out_shape=shapes[0] if one else tuple(shapes),
         in_specs=list(specs),
-        out_specs=VMEM if one else tuple(VMEM for _ in shapes),
+        out_specs=spaces or (VMEM if one else tuple(VMEM for _ in shapes)),
         scratch_shapes=list(scratch),
         compiler_params=VM,
         name=name,
@@ -53,12 +53,15 @@
     core = lax.axis_index("c")
     for r, (idx, blocks) in enumerate(((my_idx, mine), (peer_idx, peer))):
         acc = jnp.zeros((FL, B), F32)
-        for s in range(K):
-            owner = idx[s]
-            use = jnp.logical_and(owner % NC == core, s < idx[K])
-            got = xg[(owner // NC) % NP, owner // (NC * NP)]
-            got = jnp.where(use, got, jnp.zeros_like(got))
-            acc = acc + dot(got, blocks[s * B : (s + 1) * B, :], 1, 1)
+        for s in range(0, K, 2):
+            pair = []
+            for q in range(s, s + 2):
+                owner = idx[q]
+                use = jnp.logical_and(owner % NC == core, q < idx[K])
+                got = xg[(owner // NC) % NP, owner // (NC * NP)]
+                pair.append(jnp.where(use, got, jnp.zeros_like(got)))
+            vals = [blocks[q * B : (q + 1) * B, :] for q in range(s, s + 2)]
+            acc = acc + dot(jnp.concatenate(pair, axis=1), jnp.concatenate(vals, axis=1), 1, 1)
         out[r] = acc
 
 
@@ -76,7 +79,7 @@
             out[y, C_AT + c * HL : C_AT + (c + 1) * HL, :] = cot.astype(BF)
 
 
-def back_kernel(idx_a, idx_b, got, mine, peer, out_t, out, term, hidden, my_idx, peer_idx, sems):
+def back_kernel(idx_a, idx_b, got, mine, peer, out_t, out, term, hidden, kept, my_idx, peer_idx, sems):
     copies = [
         pltpu.make_async_copy(src, dst, sems.at[i])
         for i, (src, dst) in enumerate(((idx_a, my_idx), (idx_b, peer_idx)))
@@ -106,7 +109,7 @@
 
                 @pl.when(jnp.logical_and(core == c, y_at == 2 * h + q))
                 def _():
-                    out_t[...] = val[q * HL : (q + 1) * HL, c * B : (c + 1) * B]
+                    kept[...] = val[q * HL : (q + 1) * HL, c * B : (c + 1) * B]
 
         cot = jnp.concatenate(
             [
@@ -121,6 +124,8 @@
         grad = (cot.astype(F32) * der).astype(BF)
         hidden[h] = grad
         back = back + dot(got[y_at, rows, :], grad, 1, 0)
+    leave = pltpu.make_async_copy(kept, out_t, sems.at[2])
+    leave.start()
     gw = dot(own, hidden[core], 1, 1).astype(BF)
     back = back.astype(BF)
     for copy in copies:
@@ -139,6 +144,7 @@
         for z in range(NZ):
             out[x, z * FL : (z + 1) * FL, :] = term[x * NZ + z].astype(BF)
         out[x, NZ * FL :, :] = gw
+    leave.wait()
 
 
 def sum_kernel(got, out):
@@ -202,8 +208,10 @@
         "back",
         [(HBM, my_idx), (HBM, peer_idx), (VMEM, ride), (VMEM, mine), (VMEM, peer)],
         [pltpu.VMEM((NP * NZ + 1, FL, B), F32), pltpu.VMEM((2, B, NC * B), BF)]
+        + [pltpu.VMEM((HL, B), BF)]
         + [pltpu.SMEM((K + 1,), jnp.int32)] * 2
-        + [pltpu.SemaphoreType.DMA((2,))],
+        + [pltpu.SemaphoreType.DMA((3,))],
+        (HBM, VMEM),
     )
     with jax.named_scope("scatter_x"):
         term = lax.all_to_all(term, ("w", "x"), 0, 0, tiled=True)

time: 93.8 us -> 93.1 us (level)
  no operation moved by 1% of the time
where the time goes in v7:
time: 93.1 us; the launch traced here: 92.6 us
  blocking collectives  75.7 us (81%)
  starting transfers between devices  9.15 us (10%)
  Pallas kernels  3.18 us (3%)
  local copies, waits for them, and re-layouts  1.62 us (2%)
  waiting for transfers between devices  1.47 us (2%)
  between operations  1.35 us (1%)
    all_to_all x1, blocking collectives, local(): lax.all_to_all(jnp.broadcast_to(x_t, (NZ, FL, B)), 'z', 0, 0, tiled=True)  27.6 us
    all_to_all x1, blocking collectives, local(): term = lax.all_to_all(term, 'z', 0, 0, tiled=True)  15.4 us
    all_to_all x1, blocking collectives, local(): term = lax.all_to_all(term, ('w', 'x'), 0, 0, tiled=True)  11.4 us
    all_to_all x1, blocking collectives, local(): ride = lax.all_to_all(ride, 'y', 0, 0, tiled=True)  9.82 us
    all_gather x1, blocking collectives, local(): halves = lax.all_gather(half, 'c', axis=0, tiled=False)  5.82 us
    all_gather x1, blocking collectives, local(): parts = lax.all_gather(parts, 'c', axis=0, tiled=False)  5.6 us
    ppermute x1, starting transfers between devices, local(): peer = lax.ppermute(mine, 'c', [(0, 1), (1, 0)])  4.89 us
    all_to_all x1, starting transfers between devices, local(): lax.all_to_all(jnp.broadcast_to(a, (NP, NZ, FL, B)), ('w', 'x'), 0, 0, ti...  4.26 us
  transfers between devices with their start and end apart: 2, of which 1 were waited for; matrix products, arithmetic and copies ran while one was open for 0% of the time, Pallas kernels for 0%

profile of v7, /device:TPU:1, one launch (start us, length us, event | category | flops | bytes accessed | tf_op | source)
XLA Modules:
  0.0 92.6 jit_solution(15993693872532360316)
XLA Ops:
  0.6 0.7 broadcast_in_dim.10
  1.3 27.6 %all_to_all.25 = bf16[8,32,128]{2,1,0:T(8,128)(2,1)S(1)} all-to-all(bf16[8,32,128]{2,1,0:T(8,128)(2,1)S(1)} %broadcast_in_dim.10), channel_id=1, replica_groups=mesh['z'=8,'w'=2,'x'=4,'c'=2,'y'=4] {'z'}, dimensions={0} | all-to-all | bytes 131072 | tf_op jit(solution)/shard_map/gather_x/all_to_all | solution.py:170
  29.0 0.9 broadcast_in_dim.11
  29.9 0.0 copy-start.3
  29.9 0.0 copy-start
  29.9 4.3 %all-to-all-start.1 = ((bf16[8,8,32,128]{3,2,1,0:T(8,128)(2,1)}), bf16[8,8,32,128]{3,2,1,0:T(8,128)(2,1)S(1)}, u32[]{:S(2)}, u32[]{:S(2)}) async-start(bf16[8,8,32,128]{3,2,1,0:T(8,128)(2,1)} %broadcast_in_dim.11), calls=%async_computation.1 | async-start | bytes 1048576 | tf_op jit(solution)/shard_map/gather_x/all_to_all | solution.py:186
  34.1 0.0 copy-start.1
  34.8 0.0 copy-done.3
  34.8 0.1 pad_add_fusion
  34.9 0.0 copy-done
  34.9 0.0 copy-done.1
  34.9 0.1 pack.1.mine
  35.0 4.9 %collective-permute-start = (bf16[2128,128]{1,0:T(8,128)(2,1)S(1)}, bf16[2128,128]{1,0:T(8,128)(2,1)S(1)}, u32[]{:S(2)}, u32[]{:S(2)}) collective-permute-start(bf16[2128,128]{1,0:T(8,128)(2,1)S(1)} %pack.1.mine), channel_id=1, source_target_pairs={{0,4},{4,0},{1,5},{5,1},{2,6},{6,2},{3,7},{7,3},{8,12},{12,8},{9,1... | collective-permute-start | bytes 1634312 | tf_op jit(solution)/shard_map/swap_core/ppermute | solution.py:184
  39.9 0.1 fusion.1.my_idx.idx_a
  40.0 1.5 %collective-permute-done.peer = bf16[2128,128]{1,0:T(8,128)(2,1)S(1)} collective-permute-done((bf16[2128,128]{1,0:T(8,128)(2,1)S(1)}, bf16[2128,128]{1,0:T(8,128)(2,1)S(1)}, u32[]{:S(2)}, u32[]{:S(2)}) %collective-permute-start) | collective-permute-done | bytes 544800 | tf_op jit(solution)/shard_map/swap_core/ppermute | solution.py:184
  41.4 0.0 all-to-all-done.1.xg
  41.4 1.1 %agg.1 = f32[2,32,128]{2,1,0:T(8,128)S(1)} custom-call(s32[17]{0:T(128)S(1)} %fusion.1.my_idx.idx_a, s32[17]{0:T(128)S(1)} %fusion.peer_idx.idx_b, bf16[2128,128]{1,0:T(8,128)(2,1)S(1)} %pack.1.mine, bf16[2128,128]{1,0:T(8,128)(2,1)S(1)} %collective-permute-done.peer, bf16[8,8,32,128]{3,2,1,0:T(8,128)(2,1)S(1)} %all-to-all-done.1.xg), custom_call_target="tpu_custom_call" | custom-call | tf_op jit(solution)/shard_map/agg/pallas_call | solution.py:31
  42.5 0.0 copy-start.2
  42.5 5.6 %all-gather = f32[4,32,128]{2,1,0:T(8,128)S(1)} all-gather(f32[2,32,128]{2,1,0:T(8,128)S(1)} %agg.1), channel_id=2, replica_groups=mesh['z'=8,'w'=2,'x'=4,'c'=2,'y'=4] {'c'}, dimensions={0}, use_global_device_ids=true | all-gather | bytes 98304 | tf_op jit(solution)/shard_map/pair_agg/all_gather | solution.py:196
  48.1 0.0 copy-done.2
  48.1 9.8 %all_to_all.26.got = bf16[4,256,128]{2,1,0:T(8,128)(2,1)S(1)} all-to-all(bf16[4,256,128]{2,1,0:T(8,128)(2,1)S(1)} %ride.1), channel_id=1, replica_groups=mesh['z'=8,'w'=2,'x'=4,'c'=2,'y'=4] {'y'}, dimensions={0} | all-to-all | bytes 524288 | tf_op jit(solution)/shard_map/share_agg/all_to_all | solution.py:204
  58.0 1.3 %back.1 = (bf16[64,128]{1,0:T(8,128)(2,1)}, bf16[8,288,128]{2,1,0:T(8,128)(2,1)S(1)}) custom-call(s32[17]{0:T(128)S(1)} %fusion.1.my_idx.idx_a, s32[17]{0:T(128)S(1)} %fusion.peer_idx.idx_b, bf16[4,256,128]{2,1,0:T(8,128)(2,1)S(1)} %all_to_all.26.got, bf16[2128,128]{1,0:T(8,128)(2,1)S(1)} %pack.1.mine, bf16[2128,128]{1,0:T(8,128)(2,1)S(1)} %collective-permute-done.peer), custom_call_target="tpu_custom_call" | custom-call | tf_op jit(solution)/shard_map/back/pallas_call | solution.py:31
  59.2 11.4 %all_to_all.27.got = bf16[8,288,128]{2,1,0:T(8,128)(2,1)S(1)} all-to-all(bf16[8,288,128]{2,1,0:T(8,128)(2,1)S(1)} %get-tuple-element.8), channel_id=1, replica_groups=mesh['z'=8,'w'=2,'x'=4,'c'=2,'y'=4] {'w','x'}, dimensions={0} | all-to-all | bytes 1179648 | tf_op jit(solution)/shard_map/scatter_x/all_to_all | solution.py:217
  70.6 0.1 sum_x.1
  70.7 15.4 %all_to_all.28.got = bf16[8,64,128]{2,1,0:T(8,128)(2,1)S(1)} all-to-all(bf16[8,64,128]{2,1,0:T(8,128)(2,1)S(1)} %sum_x.1), channel_id=1, replica_groups=mesh['z'=8,'w'=2,'x'=4,'c'=2,'y'=4] {'z'}, dimensions={0} | all-to-all | bytes 262144 | tf_op jit(solution)/shard_map/scatter_z/all_to_all | solution.py:220
  86.1 5.8 %all-gather.1 = f32[64,128]{1,0:T(8,128)S(1)} all-gather(f32[32,128]{1,0:T(8,128)S(1)} %half.1), channel_id=3, replica_groups=mesh['z'=8,'w'=2,'x'=4,'c'=2,'y'=4] {'c'}, dimensions={0}, use_global_device_ids=true | all-gather | bytes 49152 | tf_op jit(solution)/shard_map/join_w/all_gather | solution.py:223
  92.0 0.6 last.1
  (4 shorter events, 0.1 us)
Async XLA Ops:
  29.9 4.9 %copy-start.3 = (s32[1,16]{1,0:T(1,128)S(1)}, s32[1,16]{1,0:T(1,128)}, u32[]{:S(2)}) copy-start(s32[1,16]{1,0:T(1,128)} %param.8) | copy-start | bytes 196
  29.9 5.0 %copy-start = (bf16[1,16,128,128]{3,2,1,0:T(8,128)(2,1)S(1)}, bf16[1,16,128,128]{3,2,1,0:T(8,128)(2,1)}, u32[]{:S(2)}) copy-start(bf16[1,16,128,128]{3,2,1,0:T(8,128)(2,1)} %param.10) | copy-start | bytes 1572868
  29.9 11.6 %all-to-all-start.1 = ((bf16[8,8,32,128]{3,2,1,0:T(8,128)(2,1)}), bf16[8,8,32,128]{3,2,1,0:T(8,128)(2,1)S(1)}, u32[]{:S(2)}, u32[]{:S(2)}) async-start(bf16[8,8,32,128]{3,2,1,0:T(8,128)(2,1)} %broadcast_in_dim.11), calls=%async_computation.1 | async-start | bytes 1048576 | tf_op jit(solution)/shard_map/gather_x/all_to_all | solution.py:186
  34.1 0.8 copy-start.1
  35.0 6.4 %collective-permute-start = (bf16[2128,128]{1,0:T(8,128)(2,1)S(1)}, bf16[2128,128]{1,0:T(8,128)(2,1)S(1)}, u32[]{:S(2)}, u32[]{:S(2)}) collective-permute-start(bf16[2128,128]{1,0:T(8,128)(2,1)S(1)} %pack.1.mine), channel_id=1, source_target_pairs={{0,4},{4,0},{1,5},{5,1},{2,6},{6,2},{3,7},{7,3},{8,12},{12,8},{9,1... | collective-permute-start | bytes 1634312 | tf_op jit(solution)/shard_map/swap_core/ppermute | solution.py:184
  42.5 5.6 %copy-start.2 = (bf16[32,256]{1,0:T(8,128)(2,1)S(1)}, bf16[32,256]{1,0:T(8,128)(2,1)}, u32[]{:S(2)}) copy-start(bf16[32,256]{1,0:T(8,128)(2,1)} %weight.1) | copy-start | bytes 49156

commit v8 on v7

--- a/solution.py
+++ b/solution.py
@@ -101,9 +101,10 @@
         rows = slice(W_AT + h * FL, W_AT + (h + 1) * FL)
         w = jnp.concatenate([got[y, rows, :] for y in range(NY)], axis=0)
         pre = dot(w, agg, 0, 0)
-        t = jnp.tanh(C0 * (pre + C1 * (pre * pre * pre)))
-        val = (0.5 * pre * (1.0 + t)).astype(BF)
-        der = 0.5 * (1.0 + t) + 0.5 * pre * (1.0 - t * t) * (C0 * (1.0 + 3.0 * C1 * (pre * pre)))
+        sq = pre * pre
+        u = 0.5 + 0.5 * jnp.tanh(pre * (C0 + (C0 * C1) * sq))
+        val = (pre * u).astype(BF)
+        der = u + (pre * (u - u * u)) * (2.0 * C0 + (6.0 * C0 * C1) * sq)
         for c in range(NC):
             for q in range(2):
 

time: 93.1 us -> 93.1 us (level)
  no operation moved by 1% of the time
where the time goes in v8:
time: 93.1 us; the launch traced here: 92.6 us
  blocking collectives  75.7 us (81%)
  starting transfers between devices  9.15 us (10%)
  Pallas kernels  3.15 us (3%)
  local copies, waits for them, and re-layouts  1.62 us (2%)
  waiting for transfers between devices  1.47 us (2%)
  between operations  1.35 us (1%)
    all_to_all x1, blocking collectives, local(): lax.all_to_all(jnp.broadcast_to(x_t, (NZ, FL, B)), 'z', 0, 0, tiled=True)  27.6 us
    all_to_all x1, blocking collectives, local(): term = lax.all_to_all(term, 'z', 0, 0, tiled=True)  15.4 us
    all_to_all x1, blocking collectives, local(): term = lax.all_to_all(term, ('w', 'x'), 0, 0, tiled=True)  11.4 us
    all_to_all x1, blocking collectives, local(): ride = lax.all_to_all(ride, 'y', 0, 0, tiled=True)  9.82 us
    all_gather x1, blocking collectives, local(): halves = lax.all_gather(half, 'c', axis=0, tiled=False)  5.81 us
    all_gather x1, blocking collectives, local(): parts = lax.all_gather(parts, 'c', axis=0, tiled=False)  5.6 us
    ppermute x1, starting transfers between devices, local(): peer = lax.ppermute(mine, 'c', [(0, 1), (1, 0)])  4.89 us
    all_to_all x1, starting transfers between devices, local(): lax.all_to_all(jnp.broadcast_to(a, (NP, NZ, FL, B)), ('w', 'x'), 0, 0, ti...  4.26 us
  transfers between devices with their start and end apart: 2, of which 1 were waited for; matrix products, arithmetic and copies ran while one was open for 0% of the time, Pallas kernels for 0%

profile of v8, /device:TPU:1, one launch (start us, length us, event | category | flops | bytes accessed | tf_op | source)
XLA Modules:
  0.0 92.6 jit_solution(1833920406011524101)
XLA Ops:
  0.6 0.7 broadcast_in_dim.10
  1.3 27.6 %all_to_all.25 = bf16[8,32,128]{2,1,0:T(8,128)(2,1)S(1)} all-to-all(bf16[8,32,128]{2,1,0:T(8,128)(2,1)S(1)} %broadcast_in_dim.10), channel_id=1, replica_groups=mesh['z'=8,'w'=2,'x'=4,'c'=2,'y'=4] {'z'}, dimensions={0} | all-to-all | bytes 131072 | tf_op jit(solution)/shard_map/gather_x/all_to_all | solution.py:171
  29.0 0.9 broadcast_in_dim.11
  29.9 0.0 copy-start.3
  29.9 0.0 copy-start
  29.9 4.3 %all-to-all-start.1 = ((bf16[8,8,32,128]{3,2,1,0:T(8,128)(2,1)}), bf16[8,8,32,128]{3,2,1,0:T(8,128)(2,1)S(1)}, u32[]{:S(2)}, u32[]{:S(2)}) async-start(bf16[8,8,32,128]{3,2,1,0:T(8,128)(2,1)} %broadcast_in_dim.11), calls=%async_computation.1 | async-start | bytes 1048576 | tf_op jit(solution)/shard_map/gather_x/all_to_all | solution.py:187
  34.1 0.0 copy-start.1
  34.8 0.0 copy-done.3
  34.8 0.1 pad_add_fusion
  34.9 0.0 copy-done
  34.9 0.0 copy-done.1
  34.9 0.1 pack.1.mine
  35.0 4.9 %collective-permute-start = (bf16[2128,128]{1,0:T(8,128)(2,1)S(1)}, bf16[2128,128]{1,0:T(8,128)(2,1)S(1)}, u32[]{:S(2)}, u32[]{:S(2)}) collective-permute-start(bf16[2128,128]{1,0:T(8,128)(2,1)S(1)} %pack.1.mine), channel_id=1, source_target_pairs={{0,4},{4,0},{1,5},{5,1},{2,6},{6,2},{3,7},{7,3},{8,12},{12,8},{9,1... | collective-permute-start | bytes 1634312 | tf_op jit(solution)/shard_map/swap_core/ppermute | solution.py:185
  39.9 0.1 fusion.1.my_idx.idx_a
  40.0 1.5 %collective-permute-done.peer = bf16[2128,128]{1,0:T(8,128)(2,1)S(1)} collective-permute-done((bf16[2128,128]{1,0:T(8,128)(2,1)S(1)}, bf16[2128,128]{1,0:T(8,128)(2,1)S(1)}, u32[]{:S(2)}, u32[]{:S(2)}) %collective-permute-start) | collective-permute-done | bytes 544800 | tf_op jit(solution)/shard_map/swap_core/ppermute | solution.py:185
  41.4 0.0 all-to-all-done.1.xg
  41.4 1.1 %agg.1 = f32[2,32,128]{2,1,0:T(8,128)S(1)} custom-call(s32[17]{0:T(128)S(1)} %fusion.1.my_idx.idx_a, s32[17]{0:T(128)S(1)} %fusion.peer_idx.idx_b, bf16[2128,128]{1,0:T(8,128)(2,1)S(1)} %pack.1.mine, bf16[2128,128]{1,0:T(8,128)(2,1)S(1)} %collective-permute-done.peer, bf16[8,8,32,128]{3,2,1,0:T(8,128)(2,1)S(1)} %all-to-all-done.1.xg), custom_call_target="tpu_custom_call" | custom-call | tf_op jit(solution)/shard_map/agg/pallas_call | solution.py:31
  42.5 0.0 copy-start.2
  42.5 5.6 %all-gather = f32[4,32,128]{2,1,0:T(8,128)S(1)} all-gather(f32[2,32,128]{2,1,0:T(8,128)S(1)} %agg.1), channel_id=2, replica_groups=mesh['z'=8,'w'=2,'x'=4,'c'=2,'y'=4] {'c'}, dimensions={0}, use_global_device_ids=true | all-gather | bytes 98304 | tf_op jit(solution)/shard_map/pair_agg/all_gather | solution.py:197
  48.1 0.0 copy-done.2
  48.1 9.8 %all_to_all.26.got = bf16[4,256,128]{2,1,0:T(8,128)(2,1)S(1)} all-to-all(bf16[4,256,128]{2,1,0:T(8,128)(2,1)S(1)} %ride.1), channel_id=1, replica_groups=mesh['z'=8,'w'=2,'x'=4,'c'=2,'y'=4] {'y'}, dimensions={0} | all-to-all | bytes 524288 | tf_op jit(solution)/shard_map/share_agg/all_to_all | solution.py:205
  58.0 1.2 %back.1 = (bf16[64,128]{1,0:T(8,128)(2,1)}, bf16[8,288,128]{2,1,0:T(8,128)(2,1)S(1)}) custom-call(s32[17]{0:T(128)S(1)} %fusion.1.my_idx.idx_a, s32[17]{0:T(128)S(1)} %fusion.peer_idx.idx_b, bf16[4,256,128]{2,1,0:T(8,128)(2,1)S(1)} %all_to_all.26.got, bf16[2128,128]{1,0:T(8,128)(2,1)S(1)} %pack.1.mine, bf16[2128,128]{1,0:T(8,128)(2,1)S(1)} %collective-permute-done.peer), custom_call_target="tpu_custom_call" | custom-call | tf_op jit(solution)/shard_map/back/pallas_call | solution.py:31
  59.2 11.4 %all_to_all.27.got = bf16[8,288,128]{2,1,0:T(8,128)(2,1)S(1)} all-to-all(bf16[8,288,128]{2,1,0:T(8,128)(2,1)S(1)} %get-tuple-element.8), channel_id=1, replica_groups=mesh['z'=8,'w'=2,'x'=4,'c'=2,'y'=4] {'w','x'}, dimensions={0} | all-to-all | bytes 1179648 | tf_op jit(solution)/shard_map/scatter_x/all_to_all | solution.py:218
  70.6 0.1 sum_x.1
  70.7 15.4 %all_to_all.28.got = bf16[8,64,128]{2,1,0:T(8,128)(2,1)S(1)} all-to-all(bf16[8,64,128]{2,1,0:T(8,128)(2,1)S(1)} %sum_x.1), channel_id=1, replica_groups=mesh['z'=8,'w'=2,'x'=4,'c'=2,'y'=4] {'z'}, dimensions={0} | all-to-all | bytes 262144 | tf_op jit(solution)/shard_map/scatter_z/all_to_all | solution.py:221
  86.1 5.8 %all-gather.1 = f32[64,128]{1,0:T(8,128)S(1)} all-gather(f32[32,128]{1,0:T(8,128)S(1)} %half.1), channel_id=3, replica_groups=mesh['z'=8,'w'=2,'x'=4,'c'=2,'y'=4] {'c'}, dimensions={0}, use_global_device_ids=true | all-gather | bytes 49152 | tf_op jit(solution)/shard_map/join_w/all_gather | solution.py:224
  91.9 0.6 last.1
  (4 shorter events, 0.1 us)
Async XLA Ops:
  29.9 4.9 %copy-start.3 = (s32[1,16]{1,0:T(1,128)S(1)}, s32[1,16]{1,0:T(1,128)}, u32[]{:S(2)}) copy-start(s32[1,16]{1,0:T(1,128)} %param.8) | copy-start | bytes 196
  29.9 5.0 %copy-start = (bf16[1,16,128,128]{3,2,1,0:T(8,128)(2,1)S(1)}, bf16[1,16,128,128]{3,2,1,0:T(8,128)(2,1)}, u32[]{:S(2)}) copy-start(bf16[1,16,128,128]{3,2,1,0:T(8,128)(2,1)} %param.10) | copy-start | bytes 1572868
  29.9 11.6 %all-to-all-start.1 = ((bf16[8,8,32,128]{3,2,1,0:T(8,128)(2,1)}), bf16[8,8,32,128]{3,2,1,0:T(8,128)(2,1)S(1)}, u32[]{:S(2)}, u32[]{:S(2)}) async-start(bf16[8,8,32,128]{3,2,1,0:T(8,128)(2,1)} %broadcast_in_dim.11), calls=%async_computation.1 | async-start | bytes 1048576 | tf_op jit(solution)/shard_map/gather_x/all_to_all | solution.py:187
  34.1 0.8 copy-start.1
  35.0 6.4 %collective-permute-start = (bf16[2128,128]{1,0:T(8,128)(2,1)S(1)}, bf16[2128,128]{1,0:T(8,128)(2,1)S(1)}, u32[]{:S(2)}, u32[]{:S(2)}) collective-permute-start(bf16[2128,128]{1,0:T(8,128)(2,1)S(1)} %pack.1.mine), channel_id=1, source_target_pairs={{0,4},{4,0},{1,5},{5,1},{2,6},{6,2},{3,7},{7,3},{8,12},{12,8},{9,1... | collective-permute-start | bytes 1634312 | tf_op jit(solution)/shard_map/swap_core/ppermute | solution.py:185
  42.5 5.6 %copy-start.2 = (bf16[32,256]{1,0:T(8,128)(2,1)S(1)}, bf16[32,256]{1,0:T(8,128)(2,1)}, u32[]{:S(2)}) copy-start(bf16[32,256]{1,0:T(8,128)(2,1)} %weight.1) | copy-start | bytes 49156

commit v9 on v8

--- a/solution.py
+++ b/solution.py
@@ -105,13 +105,7 @@
         u = 0.5 + 0.5 * jnp.tanh(pre * (C0 + (C0 * C1) * sq))
         val = (pre * u).astype(BF)
         der = u + (pre * (u - u * u)) * (2.0 * C0 + (6.0 * C0 * C1) * sq)
-        for c in range(NC):
-            for q in range(2):
-
-                @pl.when(jnp.logical_and(core == c, y_at == 2 * h + q))
-                def _():
-                    kept[...] = val[q * HL : (q + 1) * HL, c * B : (c + 1) * B]
-
+        kept[h * B : (h + 1) * B, :] = val
         cot = jnp.concatenate(
             [
                 jnp.concatenate(
@@ -125,7 +119,9 @@
         grad = (cot.astype(F32) * der).astype(BF)
         hidden[h] = grad
         back = back + dot(got[y_at, rows, :], grad, 1, 0)
-    leave = pltpu.make_async_copy(kept, out_t, sems.at[2])
+    rows = pl.ds(pl.multiple_of(y_at * HL, HL), HL)
+    lanes = pl.ds(pl.multiple_of(core * B, B), B)
+    leave = pltpu.make_async_copy(kept.at[rows, lanes], out_t, sems.at[2])
     leave.start()
     gw = dot(own, hidden[core], 1, 1).astype(BF)
     back = back.astype(BF)
@@ -209,7 +205,7 @@
         "back",
         [(HBM, my_idx), (HBM, peer_idx), (VMEM, ride), (VMEM, mine), (VMEM, peer)],
         [pltpu.VMEM((NP * NZ + 1, FL, B), F32), pltpu.VMEM((2, B, NC * B), BF)]
-        + [pltpu.VMEM((HL, B), BF)]
+        + [pltpu.VMEM((2 * B, NC * B), BF)]
         + [pltpu.SMEM((K + 1,), jnp.int32)] * 2
         + [pltpu.SemaphoreType.DMA((3,))],
         (HBM, VMEM),

time: 93.1 us -> 92.9 us (level)
  no operation moved by 1% of the time
where the time goes in v9:
time: 92.9 us; the launch traced here: 92.4 us
  blocking collectives  75.7 us (81%)
  starting transfers between devices  9.15 us (10%)
  Pallas kernels  3.01 us (3%)
  local copies, waits for them, and re-layouts  1.62 us (2%)
  waiting for transfers between devices  1.47 us (2%)
  between operations  1.35 us (1%)
    all_to_all x1, blocking collectives, local(): lax.all_to_all(jnp.broadcast_to(x_t, (NZ, FL, B)), 'z', 0, 0, tiled=True)  27.6 us
    all_to_all x1, blocking collectives, local(): term = lax.all_to_all(term, 'z', 0, 0, tiled=True)  15.4 us
    all_to_all x1, blocking collectives, local(): term = lax.all_to_all(term, ('w', 'x'), 0, 0, tiled=True)  11.3 us
    all_to_all x1, blocking collectives, local(): ride = lax.all_to_all(ride, 'y', 0, 0, tiled=True)  9.82 us
    all_gather x1, blocking collectives, local(): halves = lax.all_gather(half, 'c', axis=0, tiled=False)  5.82 us
    all_gather x1, blocking collectives, local(): parts = lax.all_gather(parts, 'c', axis=0, tiled=False)  5.6 us
    ppermute x1, starting transfers between devices, local(): peer = lax.ppermute(mine, 'c', [(0, 1), (1, 0)])  4.89 us
    all_to_all x1, starting transfers between devices, local(): lax.all_to_all(jnp.broadcast_to(a, (NP, NZ, FL, B)), ('w', 'x'), 0, 0, ti...  4.26 us
  transfers between devices with their start and end apart: 2, of which 1 were waited for; matrix products, arithmetic and copies ran while one was open for 0% of the time, Pallas kernels for 0%

profile of v9, /device:TPU:1, one launch (start us, length us, event | category | flops | bytes accessed | tf_op | source)
XLA Modules:
  0.0 92.4 jit_solution(6173147779496481651)
XLA Ops:
  0.6 0.7 broadcast_in_dim.10
  1.3 27.6 %all_to_all.25 = bf16[8,32,128]{2,1,0:T(8,128)(2,1)S(1)} all-to-all(bf16[8,32,128]{2,1,0:T(8,128)(2,1)S(1)} %broadcast_in_dim.10), channel_id=1, replica_groups=mesh['z'=8,'w'=2,'x'=4,'c'=2,'y'=4] {'z'}, dimensions={0} | all-to-all | bytes 131072 | tf_op jit(solution)/shard_map/gather_x/all_to_all | solution.py:167
  29.0 0.9 broadcast_in_dim.11
  29.9 0.0 copy-start.3
  29.9 0.0 copy-start
  29.9 4.3 %all-to-all-start.1 = ((bf16[8,8,32,128]{3,2,1,0:T(8,128)(2,1)}), bf16[8,8,32,128]{3,2,1,0:T(8,128)(2,1)S(1)}, u32[]{:S(2)}, u32[]{:S(2)}) async-start(bf16[8,8,32,128]{3,2,1,0:T(8,128)(2,1)} %broadcast_in_dim.11), calls=%async_computation.1 | async-start | bytes 1048576 | tf_op jit(solution)/shard_map/gather_x/all_to_all | solution.py:183
  34.1 0.0 copy-start.1
  34.8 0.0 copy-done.3
  34.8 0.1 pad_add_fusion
  34.9 0.0 copy-done
  34.9 0.0 copy-done.1
  34.9 0.1 pack.1.mine
  35.0 4.9 %collective-permute-start = (bf16[2128,128]{1,0:T(8,128)(2,1)S(1)}, bf16[2128,128]{1,0:T(8,128)(2,1)S(1)}, u32[]{:S(2)}, u32[]{:S(2)}) collective-permute-start(bf16[2128,128]{1,0:T(8,128)(2,1)S(1)} %pack.1.mine), channel_id=1, source_target_pairs={{0,4},{4,0},{1,5},{5,1},{2,6},{6,2},{3,7},{7,3},{8,12},{12,8},{9,1... | collective-permute-start | bytes 1634312 | tf_op jit(solution)/shard_map/swap_core/ppermute | solution.py:181
  39.9 0.1 fusion.1.my_idx.idx_a
  40.0 1.5 %collective-permute-done.peer = bf16[2128,128]{1,0:T(8,128)(2,1)S(1)} collective-permute-done((bf16[2128,128]{1,0:T(8,128)(2,1)S(1)}, bf16[2128,128]{1,0:T(8,128)(2,1)S(1)}, u32[]{:S(2)}, u32[]{:S(2)}) %collective-permute-start) | collective-permute-done | bytes 544800 | tf_op jit(solution)/shard_map/swap_core/ppermute | solution.py:181
  41.4 0.0 all-to-all-done.1.xg
  41.4 1.1 %agg.1 = f32[2,32,128]{2,1,0:T(8,128)S(1)} custom-call(s32[17]{0:T(128)S(1)} %fusion.1.my_idx.idx_a, s32[17]{0:T(128)S(1)} %fusion.peer_idx.idx_b, bf16[2128,128]{1,0:T(8,128)(2,1)S(1)} %pack.1.mine, bf16[2128,128]{1,0:T(8,128)(2,1)S(1)} %collective-permute-done.peer, bf16[8,8,32,128]{3,2,1,0:T(8,128)(2,1)S(1)} %all-to-all-done.1.xg), custom_call_target="tpu_custom_call" | custom-call | tf_op jit(solution)/shard_map/agg/pallas_call | solution.py:31
  42.5 0.0 copy-start.2
  42.5 5.6 %all-gather = f32[4,32,128]{2,1,0:T(8,128)S(1)} all-gather(f32[2,32,128]{2,1,0:T(8,128)S(1)} %agg.1), channel_id=2, replica_groups=mesh['z'=8,'w'=2,'x'=4,'c'=2,'y'=4] {'c'}, dimensions={0}, use_global_device_ids=true | all-gather | bytes 98304 | tf_op jit(solution)/shard_map/pair_agg/all_gather | solution.py:193
  48.1 0.0 copy-done.2
  48.1 9.8 %all_to_all.26.got = bf16[4,256,128]{2,1,0:T(8,128)(2,1)S(1)} all-to-all(bf16[4,256,128]{2,1,0:T(8,128)(2,1)S(1)} %ride.1), channel_id=1, replica_groups=mesh['z'=8,'w'=2,'x'=4,'c'=2,'y'=4] {'y'}, dimensions={0} | all-to-all | bytes 524288 | tf_op jit(solution)/shard_map/share_agg/all_to_all | solution.py:201
  58.0 1.1 %back.1 = (bf16[64,128]{1,0:T(8,128)(2,1)}, bf16[8,288,128]{2,1,0:T(8,128)(2,1)S(1)}) custom-call(s32[17]{0:T(128)S(1)} %fusion.1.my_idx.idx_a, s32[17]{0:T(128)S(1)} %fusion.peer_idx.idx_b, bf16[4,256,128]{2,1,0:T(8,128)(2,1)S(1)} %all_to_all.26.got, bf16[2128,128]{1,0:T(8,128)(2,1)S(1)} %pack.1.mine, bf16[2128,128]{1,0:T(8,128)(2,1)S(1)} %collective-permute-done.peer), custom_call_target="tpu_custom_call" | custom-call | tf_op jit(solution)/shard_map/back/pallas_call | solution.py:31
  59.1 11.3 %all_to_all.27.got = bf16[8,288,128]{2,1,0:T(8,128)(2,1)S(1)} all-to-all(bf16[8,288,128]{2,1,0:T(8,128)(2,1)S(1)} %get-tuple-element.8), channel_id=1, replica_groups=mesh['z'=8,'w'=2,'x'=4,'c'=2,'y'=4] {'w','x'}, dimensions={0} | all-to-all | bytes 1179648 | tf_op jit(solution)/shard_map/scatter_x/all_to_all | solution.py:214
  70.4 0.1 sum_x.1
  70.5 15.4 %all_to_all.28.got = bf16[8,64,128]{2,1,0:T(8,128)(2,1)S(1)} all-to-all(bf16[8,64,128]{2,1,0:T(8,128)(2,1)S(1)} %sum_x.1), channel_id=1, replica_groups=mesh['z'=8,'w'=2,'x'=4,'c'=2,'y'=4] {'z'}, dimensions={0} | all-to-all | bytes 262144 | tf_op jit(solution)/shard_map/scatter_z/all_to_all | solution.py:217
  86.0 5.8 %all-gather.1 = f32[64,128]{1,0:T(8,128)S(1)} all-gather(f32[32,128]{1,0:T(8,128)S(1)} %half.1), channel_id=3, replica_groups=mesh['z'=8,'w'=2,'x'=4,'c'=2,'y'=4] {'c'}, dimensions={0}, use_global_device_ids=true | all-gather | bytes 49152 | tf_op jit(solution)/shard_map/join_w/all_gather | solution.py:220
  91.8 0.6 last.1
  (4 shorter events, 0.1 us)
Async XLA Ops:
  29.9 4.9 %copy-start.3 = (s32[1,16]{1,0:T(1,128)S(1)}, s32[1,16]{1,0:T(1,128)}, u32[]{:S(2)}) copy-start(s32[1,16]{1,0:T(1,128)} %param.8) | copy-start | bytes 196
  29.9 5.0 %copy-start = (bf16[1,16,128,128]{3,2,1,0:T(8,128)(2,1)S(1)}, bf16[1,16,128,128]{3,2,1,0:T(8,128)(2,1)}, u32[]{:S(2)}) copy-start(bf16[1,16,128,128]{3,2,1,0:T(8,128)(2,1)} %param.10) | copy-start | bytes 1572868
  29.9 11.6 %all-to-all-start.1 = ((bf16[8,8,32,128]{3,2,1,0:T(8,128)(2,1)}), bf16[8,8,32,128]{3,2,1,0:T(8,128)(2,1)S(1)}, u32[]{:S(2)}, u32[]{:S(2)}) async-start(bf16[8,8,32,128]{3,2,1,0:T(8,128)(2,1)} %broadcast_in_dim.11), calls=%async_computation.1 | async-start | bytes 1048576 | tf_op jit(solution)/shard_map/gather_x/all_to_all | solution.py:183
  34.1 0.8 copy-start.1
  35.0 6.4 %collective-permute-start = (bf16[2128,128]{1,0:T(8,128)(2,1)S(1)}, bf16[2128,128]{1,0:T(8,128)(2,1)S(1)}, u32[]{:S(2)}, u32[]{:S(2)}) collective-permute-start(bf16[2128,128]{1,0:T(8,128)(2,1)S(1)} %pack.1.mine), channel_id=1, source_target_pairs={{0,4},{4,0},{1,5},{5,1},{2,6},{6,2},{3,7},{7,3},{8,12},{12,8},{9,1... | collective-permute-start | bytes 1634312 | tf_op jit(solution)/shard_map/swap_core/ppermute | solution.py:181
  42.5 5.6 %copy-start.2 = (bf16[32,256]{1,0:T(8,128)(2,1)S(1)}, bf16[32,256]{1,0:T(8,128)(2,1)}, u32[]{:S(2)}) copy-start(bf16[32,256]{1,0:T(8,128)(2,1)} %weight.1) | copy-start | bytes 49156

commit v10 on v9

--- a/solution.py
+++ b/solution.py
@@ -136,7 +136,8 @@
             use = jnp.logical_and(owner % NC == core, s < idx[K])
             at = ((owner // NC) % NP) * NZ + owner // (NC * NP)
             at = jnp.where(use, at, NP * NZ)
-            term[at] = term[at] + dot(grad, blocks[s * B : (s + 1) * B, :], 1, 0)
+            new = dot(grad, blocks[s * B : (s + 1) * B, :], 1, 0)
+            term[at] = new if r == 0 else term[at] + new
     for x in range(NP):
         for z in range(NZ):
             out[x, z * FL : (z + 1) * FL, :] = term[x * NZ + z].astype(BF)

time: 92.9 us -> 92.9 us (level)
  no operation moved by 1% of the time
where the time goes in v10:
time: 92.9 us; the launch traced here: 92.4 us
  blocking collectives  75.7 us (81%)
  starting transfers between devices  9.15 us (10%)
  Pallas kernels  3 us (3%)
  local copies, waits for them, and re-layouts  1.62 us (2%)
  waiting for transfers between devices  1.47 us (2%)
  between operations  1.35 us (1%)
    all_to_all x1, blocking collectives, local(): lax.all_to_all(jnp.broadcast_to(x_t, (NZ, FL, B)), 'z', 0, 0, tiled=True)  27.6 us
    all_to_all x1, blocking collectives, local(): term = lax.all_to_all(term, 'z', 0, 0, tiled=True)  15.4 us
    all_to_all x1, blocking collectives, local(): term = lax.all_to_all(term, ('w', 'x'), 0, 0, tiled=True)  11.4 us
    all_to_all x1, blocking collectives, local(): ride = lax.all_to_all(ride, 'y', 0, 0, tiled=True)  9.82 us
    all_gather x1, blocking collectives, local(): halves = lax.all_gather(half, 'c', axis=0, tiled=False)  5.81 us
    all_gather x1, blocking collectives, local(): parts = lax.all_gather(parts, 'c', axis=0, tiled=False)  5.6 us
    ppermute x1, starting transfers between devices, local(): peer = lax.ppermute(mine, 'c', [(0, 1), (1, 0)])  4.89 us
    all_to_all x1, starting transfers between devices, local(): lax.all_to_all(jnp.broadcast_to(a, (NP, NZ, FL, B)), ('w', 'x'), 0, 0, ti...  4.26 us
  transfers between devices with their start and end apart: 2, of which 1 were waited for; matrix products, arithmetic and copies ran while one was open for 0% of the time, Pallas kernels for 0%

profile of v10, /device:TPU:1, one launch (start us, length us, event | category | flops | bytes accessed | tf_op | source)
XLA Modules:
  0.0 92.4 jit_solution(1897603395506895386)
XLA Ops:
  0.6 0.7 broadcast_in_dim.10
  1.3 27.6 %all_to_all.25 = bf16[8,32,128]{2,1,0:T(8,128)(2,1)S(1)} all-to-all(bf16[8,32,128]{2,1,0:T(8,128)(2,1)S(1)} %broadcast_in_dim.10), channel_id=1, replica_groups=mesh['z'=8,'w'=2,'x'=4,'c'=2,'y'=4] {'z'}, dimensions={0} | all-to-all | bytes 131072 | tf_op jit(solution)/shard_map/gather_x/all_to_all | solution.py:168
  29.0 0.9 broadcast_in_dim.11
  29.9 0.0 copy-start.3
  29.9 0.0 copy-start
  29.9 4.3 %all-to-all-start.1 = ((bf16[8,8,32,128]{3,2,1,0:T(8,128)(2,1)}), bf16[8,8,32,128]{3,2,1,0:T(8,128)(2,1)S(1)}, u32[]{:S(2)}, u32[]{:S(2)}) async-start(bf16[8,8,32,128]{3,2,1,0:T(8,128)(2,1)} %broadcast_in_dim.11), calls=%async_computation.1 | async-start | bytes 1048576 | tf_op jit(solution)/shard_map/gather_x/all_to_all | solution.py:184
  34.1 0.0 copy-start.1
  34.8 0.0 copy-done.3
  34.8 0.1 pad_add_fusion
  34.9 0.0 copy-done
  34.9 0.0 copy-done.1
  34.9 0.1 pack.1.mine
  35.0 4.9 %collective-permute-start = (bf16[2128,128]{1,0:T(8,128)(2,1)S(1)}, bf16[2128,128]{1,0:T(8,128)(2,1)S(1)}, u32[]{:S(2)}, u32[]{:S(2)}) collective-permute-start(bf16[2128,128]{1,0:T(8,128)(2,1)S(1)} %pack.1.mine), channel_id=1, source_target_pairs={{0,4},{4,0},{1,5},{5,1},{2,6},{6,2},{3,7},{7,3},{8,12},{12,8},{9,1... | collective-permute-start | bytes 1634312 | tf_op jit(solution)/shard_map/swap_core/ppermute | solution.py:182
  39.9 0.1 fusion.1.my_idx.idx_a
  40.0 1.5 %collective-permute-done.peer = bf16[2128,128]{1,0:T(8,128)(2,1)S(1)} collective-permute-done((bf16[2128,128]{1,0:T(8,128)(2,1)S(1)}, bf16[2128,128]{1,0:T(8,128)(2,1)S(1)}, u32[]{:S(2)}, u32[]{:S(2)}) %collective-permute-start) | collective-permute-done | bytes 544800 | tf_op jit(solution)/shard_map/swap_core/ppermute | solution.py:182
  41.4 0.0 all-to-all-done.1.xg
  41.4 1.1 %agg.1 = f32[2,32,128]{2,1,0:T(8,128)S(1)} custom-call(s32[17]{0:T(128)S(1)} %fusion.1.my_idx.idx_a, s32[17]{0:T(128)S(1)} %fusion.peer_idx.idx_b, bf16[2128,128]{1,0:T(8,128)(2,1)S(1)} %pack.1.mine, bf16[2128,128]{1,0:T(8,128)(2,1)S(1)} %collective-permute-done.peer, bf16[8,8,32,128]{3,2,1,0:T(8,128)(2,1)S(1)} %all-to-all-done.1.xg), custom_call_target="tpu_custom_call" | custom-call | tf_op jit(solution)/shard_map/agg/pallas_call | solution.py:31
  42.5 0.0 copy-start.2
  42.5 5.6 %all-gather = f32[4,32,128]{2,1,0:T(8,128)S(1)} all-gather(f32[2,32,128]{2,1,0:T(8,128)S(1)} %agg.1), channel_id=2, replica_groups=mesh['z'=8,'w'=2,'x'=4,'c'=2,'y'=4] {'c'}, dimensions={0}, use_global_device_ids=true | all-gather | bytes 98304 | tf_op jit(solution)/shard_map/pair_agg/all_gather | solution.py:194
  48.1 0.0 copy-done.2
  48.1 9.8 %all_to_all.26.got = bf16[4,256,128]{2,1,0:T(8,128)(2,1)S(1)} all-to-all(bf16[4,256,128]{2,1,0:T(8,128)(2,1)S(1)} %ride.1), channel_id=1, replica_groups=mesh['z'=8,'w'=2,'x'=4,'c'=2,'y'=4] {'y'}, dimensions={0} | all-to-all | bytes 524288 | tf_op jit(solution)/shard_map/share_agg/all_to_all | solution.py:202
  58.0 1.1 %back.1 = (bf16[64,128]{1,0:T(8,128)(2,1)}, bf16[8,288,128]{2,1,0:T(8,128)(2,1)S(1)}) custom-call(s32[17]{0:T(128)S(1)} %fusion.1.my_idx.idx_a, s32[17]{0:T(128)S(1)} %fusion.peer_idx.idx_b, bf16[4,256,128]{2,1,0:T(8,128)(2,1)S(1)} %all_to_all.26.got, bf16[2128,128]{1,0:T(8,128)(2,1)S(1)} %pack.1.mine, bf16[2128,128]{1,0:T(8,128)(2,1)S(1)} %collective-permute-done.peer), custom_call_target="tpu_custom_call" | custom-call | tf_op jit(solution)/shard_map/back/pallas_call | solution.py:31
  59.1 11.4 %all_to_all.27.got = bf16[8,288,128]{2,1,0:T(8,128)(2,1)S(1)} all-to-all(bf16[8,288,128]{2,1,0:T(8,128)(2,1)S(1)} %get-tuple-element.8), channel_id=1, replica_groups=mesh['z'=8,'w'=2,'x'=4,'c'=2,'y'=4] {'w','x'}, dimensions={0} | all-to-all | bytes 1179648 | tf_op jit(solution)/shard_map/scatter_x/all_to_all | solution.py:215
  70.4 0.1 sum_x.1
  70.5 15.4 %all_to_all.28.got = bf16[8,64,128]{2,1,0:T(8,128)(2,1)S(1)} all-to-all(bf16[8,64,128]{2,1,0:T(8,128)(2,1)S(1)} %sum_x.1), channel_id=1, replica_groups=mesh['z'=8,'w'=2,'x'=4,'c'=2,'y'=4] {'z'}, dimensions={0} | all-to-all | bytes 262144 | tf_op jit(solution)/shard_map/scatter_z/all_to_all | solution.py:218
  86.0 5.8 %all-gather.1 = f32[64,128]{1,0:T(8,128)S(1)} all-gather(f32[32,128]{1,0:T(8,128)S(1)} %half.1), channel_id=3, replica_groups=mesh['z'=8,'w'=2,'x'=4,'c'=2,'y'=4] {'c'}, dimensions={0}, use_global_device_ids=true | all-gather | bytes 49152 | tf_op jit(solution)/shard_map/join_w/all_gather | solution.py:221
  91.8 0.6 last.1
  (4 shorter events, 0.1 us)
Async XLA Ops:
  29.9 4.9 %copy-start.3 = (s32[1,16]{1,0:T(1,128)S(1)}, s32[1,16]{1,0:T(1,128)}, u32[]{:S(2)}) copy-start(s32[1,16]{1,0:T(1,128)} %param.8) | copy-start | bytes 196
  29.9 5.0 %copy-start = (bf16[1,16,128,128]{3,2,1,0:T(8,128)(2,1)S(1)}, bf16[1,16,128,128]{3,2,1,0:T(8,128)(2,1)}, u32[]{:S(2)}) copy-start(bf16[1,16,128,128]{3,2,1,0:T(8,128)(2,1)} %param.10) | copy-start | bytes 1572868
  29.9 11.6 %all-to-all-start.1 = ((bf16[8,8,32,128]{3,2,1,0:T(8,128)(2,1)}), bf16[8,8,32,128]{3,2,1,0:T(8,128)(2,1)S(1)}, u32[]{:S(2)}, u32[]{:S(2)}) async-start(bf16[8,8,32,128]{3,2,1,0:T(8,128)(2,1)} %broadcast_in_dim.11), calls=%async_computation.1 | async-start | bytes 1048576 | tf_op jit(solution)/shard_map/gather_x/all_to_all | solution.py:184
  34.1 0.8 copy-start.1
  35.0 6.4 %collective-permute-start = (bf16[2128,128]{1,0:T(8,128)(2,1)S(1)}, bf16[2128,128]{1,0:T(8,128)(2,1)S(1)}, u32[]{:S(2)}, u32[]{:S(2)}) collective-permute-start(bf16[2128,128]{1,0:T(8,128)(2,1)S(1)} %pack.1.mine), channel_id=1, source_target_pairs={{0,4},{4,0},{1,5},{5,1},{2,6},{6,2},{3,7},{7,3},{8,12},{12,8},{9,1... | collective-permute-start | bytes 1634312 | tf_op jit(solution)/shard_map/swap_core/ppermute | solution.py:182
  42.5 5.6 %copy-start.2 = (bf16[32,256]{1,0:T(8,128)(2,1)S(1)}, bf16[32,256]{1,0:T(8,128)(2,1)}, u32[]{:S(2)}) copy-start(bf16[32,256]{1,0:T(8,128)(2,1)} %weight.1) | copy-start | bytes 49156
